TPU v7x, 512 devices: a whole 4x4x16 slice. The times are simulated.
512 devices in a mesh: lev: 4 (over y), tile: 64 (over z_lo, x, core), sec: 2 (over z_hi).
Axes of the slice: x: 4, y: 4, z: 16 (z_hi: 2, z_lo: 8; z = z_hi * 8 + z_lo), core: 2. Of those that a mesh axis runs over, the one named last changes fastest.
Arguments:
- fields: float32 [3, 64, 4, 128, 360], P(None, ('lev', 'sec'), None, 'tile'), may hold values from -6 to 6
- surface: float32 [4, 128, 360], P(None, 'tile'), may hold values from -6 to 6
- cot_fields: float32 [3, 64, 4, 128, 360], P(None, ('lev', 'sec'), None, 'tile'), may hold values from -6 to 6
- cot_surface: float32 [4, 128, 360], P(None, 'tile'), may hold values from -6 to 6
- land_sea: int32 [128, 360], P('tile'), may hold values 0 or 1
- w_in: bfloat16 [192, 384], replicated, may hold values from -0.4375 to 0.4375
- w_mid: bfloat16 [384, 384], replicated, may hold values from -0.3125 to 0.3125
- w_out: bfloat16 [384, 192], replicated, may hold values from -0.3125 to 0.3125
- bias_in: float32 [2, 384], replicated, may hold values from -4 to 4
Outputs:
- final_fields: float32 [3, 64, 4, 128, 360], P(None, ('lev', 'sec'), None, 'tile')
- final_surface: float32 [4, 128, 360], P(None, 'tile')
- fields_grad: float32 [3, 64, 4, 128, 360], P(None, ('lev', 'sec'), None, 'tile')
- surface_grad: float32 [4, 128, 360], P(None, 'tile')
- w_in_grad: float32 [192, 384], replicated
- w_mid_grad: float32 [384, 384], replicated
- w_out_grad: float32 [384, 192], replicated
- bias_grad: float32 [2, 384], replicated
Inputs may be any that keep to these rules, and one draw needn't show every extreme that they name: `land_sea`: 1 marks land, 0 sea.
All inputs are finite; a program needn't handle non-finite values. No bound on the sum of `land_sea` on one device may be relied on, other than what follows from the above.
Results may differ from a plain program's by a relative error of at most 0.005.
Values may be sent and summed in bfloat16 or wider, within the bound.
A program may use at most 64 MiB of HBM per device.

v0:
```python
import math

import jax
import jax.numpy as jnp
from jax import lax
from jax.sharding import PartitionSpec as P

NLEV = 64
STEPS = 2


TIME_STEP = 0.1
COS_FLOOR = 0.2
INV_SQRT_TWO = 1.0 / math.sqrt(2.0)
INV_SQRT_TWO_PI = 1.0 / math.sqrt(2.0 * math.pi)


def extended(value, sides, width):
    for axis, dim in sides:
        size, length = (lax.axis_size(axis), value.shape[dim])
        up = [(i, (i + 1) % size) for i in range(size - 1)]
        down = [(j, i) for i, j in up]
        last = lax.slice_in_dim(value, length - width, length, axis=dim)
        first = lax.slice_in_dim(value, 0, width, axis=dim)
        before = lax.ppermute(last, axis, up)
        after = lax.ppermute(first, axis, down)
        value = jnp.concatenate([before, value, after], axis=dim)
    return value


def carried_in(part, axis, combine, identity):
    place = lax.axis_index(axis)
    gathered = jax.tree.map(lambda a: lax.all_gather(a, axis), part)
    state = jax.tree.map(lambda a, e: jnp.zeros_like(a) + jnp.asarray(e, a.dtype), part, identity)

    def one(lap, state):
        return combine(
            state, jax.tree.map(lambda a: lax.dynamic_index_in_dim(a, lap, 0, False), gathered)
        )

    return lax.fori_loop(0, place, one, state)


def gelu_slope(values):
    cumulative = 0.5 * (1.0 + lax.erf(values * INV_SQRT_TWO))
    density = jnp.exp(-0.5 * values * values) * INV_SQRT_TWO_PI
    return cumulative + values * density


def lon_change(values, x_factor):
    return (jnp.roll(values, -1, axis=-1) - jnp.roll(values, 1, axis=-1)) * x_factor


def lat_change(values):
    padded = extended(values, (("tile", 2),), 1)
    return (padded[:, :, 2:, :] - padded[:, :, :-2, :]) * 0.5


def add_pairs(earlier, later):
    return (earlier[0] + later[0], earlier[1] + later[1])


def vertical_sums(rising_in, falling_in):
    rising_run = jnp.cumsum(rising_in, axis=0)
    falling_run = jnp.flip(jnp.cumsum(jnp.flip(falling_in, 0), axis=0), 0)
    rising_part = rising_run[-1]
    falling_part = falling_run[0]
    zeros_part = jnp.zeros_like(rising_part)
    before, falling_before = carried_in(
        (rising_part, falling_part), ("lev", "sec"), add_pairs, (zeros_part, zeros_part)
    )
    column_sum, falling_total = lax.psum((rising_part, falling_part), ("lev", "sec"))
    beyond = falling_total - falling_before - falling_part
    return (before + rising_run, beyond + falling_run, column_sum)


def on_device(fields, surface, cot_fields, cot_surface, land_sea, w_in, w_mid, w_out, bias_in):
    lev_dev = fields.shape[1]
    batch_size = fields.shape[2]
    lat_dev = fields.shape[3]
    lon_cells = fields.shape[4]
    level_shape = fields.shape
    shard_count = lax.axis_size(("lev", "sec"))
    position = lax.axis_index(("lev", "sec"))
    lat_total = lat_dev * lax.axis_size("tile")
    row_ids = (lax.axis_index("tile") * lat_dev + jnp.arange(lat_dev)).astype(jnp.float32)
    latitude = -0.5 * math.pi + (row_ids + 0.5) * (math.pi / lat_total)
    x_factor = (0.5 / jnp.maximum(jnp.cos(latitude), COS_FLOOR))[:, None]
    sin_lat = jnp.sin(latitude)[:, None]
    level_ids = (position * lev_dev + jnp.arange(lev_dev)).astype(jnp.float32)
    layer_thickness_fraction = (1.0 / (level_ids + 1.0))[:, None, None, None]
    col_count = batch_size * lat_dev * lon_cells // shard_count
    mask_all = jnp.broadcast_to(land_sea[None], (batch_size, lat_dev, lon_cells)).reshape(-1)
    mask_cols = lax.dynamic_slice_in_dim(mask_all, position * col_count, col_count)
    land_cols = (mask_cols > 0)[None, :]
    bias_cols = jnp.where(mask_cols[None, :] > 0, bias_in[1][:, None], bias_in[0][:, None])

    def to_columns(values):
        flattened = values.reshape(values.shape[0], values.shape[1], -1)
        arrived = lax.all_to_all(flattened, ("lev", "sec"), split_axis=2, concat_axis=1, tiled=True)
        return arrived.reshape(arrived.shape[0] * arrived.shape[1], arrived.shape[2])

    def to_levels(values):
        regrouped = values.reshape(level_shape[0], -1, values.shape[1])
        arrived = lax.all_to_all(regrouped, ("lev", "sec"), split_axis=1, concat_axis=2, tiled=True)
        return arrived.reshape(level_shape)

    current_fields_bundle, current_ground_pressure = (fields, surface)
    stored = []
    for instant in range(STEPS):
        x_cols = to_columns(current_fields_bundle.astype(jnp.bfloat16))
        first_pre = (
            jnp.einsum("fh,fc->hc", w_in, x_cols, preferred_element_type=jnp.float32) + bias_cols
        )
        first_act = jax.nn.gelu(first_pre, approximate=False).astype(jnp.bfloat16)
        second_pre = jnp.einsum("io,ic->oc", w_mid, first_act, preferred_element_type=jnp.float32)
        second_act = jax.nn.gelu(second_pre, approximate=False).astype(jnp.bfloat16)
        first_pre, first_act, second_pre, second_act = (
            first_pre,
            first_act,
            second_pre,
            second_act,
        )
        tendency = jnp.einsum(
            "hf,hc->fc", w_out, second_act, preferred_element_type=jnp.float32
        ).astype(jnp.bfloat16)
        zonal_velocity = current_fields_bundle[0]
        meridional_velocity = current_fields_bundle[1]
        thermal_field = current_fields_bundle[2]
        velocity_spreading = lon_change(zonal_velocity, x_factor) + lat_change(meridional_velocity)
        dynamics_prefix, dynamics_suffix, dynamics_column_sum = vertical_sums(
            velocity_spreading, layer_thickness_fraction * thermal_field
        )
        gravity_potential_elevation = dynamics_suffix + current_ground_pressure[None]
        zonal_tend = (
            -lon_change(gravity_potential_elevation, x_factor) + sin_lat * meridional_velocity
        )
        merid_tend = -lat_change(gravity_potential_elevation) - sin_lat * zonal_velocity
        temp_tend = -(dynamics_prefix / NLEV)
        dyn_fields = jnp.stack([zonal_tend, merid_tend, temp_tend])
        dyn_surface = -dynamics_column_sum / NLEV
        physics = to_levels(tendency).astype(jnp.float32)
        current_fields_bundle = current_fields_bundle + TIME_STEP * (dyn_fields + physics)
        current_ground_pressure = current_ground_pressure + TIME_STEP * dyn_surface
        stored.append((x_cols, first_pre, first_act, second_pre, second_act))
    field_bar, surface_bar = (cot_fields, cot_surface)
    gradient = (
        jnp.zeros(w_in.shape, jnp.float32),
        jnp.zeros(w_mid.shape, jnp.float32),
        jnp.zeros(w_out.shape, jnp.float32),
        jnp.zeros(bias_in.shape, jnp.float32),
    )
    for instant in reversed(range(STEPS)):
        x_cols, first_pre, first_act, second_pre, second_act = stored[instant]
        tend_bar = to_columns((TIME_STEP * field_bar).astype(jnp.bfloat16))
        second_bar = (
            jnp.einsum("hf,fc->hc", w_out, tend_bar, preferred_element_type=jnp.float32)
            * gelu_slope(second_pre)
        ).astype(jnp.bfloat16)
        first_bar = (
            jnp.einsum("io,oc->ic", w_mid, second_bar, preferred_element_type=jnp.float32)
            * gelu_slope(first_pre)
        ).astype(jnp.bfloat16)
        input_bar = jnp.einsum(
            "fh,hc->fc", w_in, first_bar, preferred_element_type=jnp.float32
        ).astype(jnp.bfloat16)
        first_wide = first_bar.astype(jnp.float32)
        zero_f = jnp.zeros((), jnp.float32)
        sea_part = jnp.sum(jnp.where(land_cols, zero_f, first_wide), axis=1)
        land_part = jnp.sum(jnp.where(land_cols, first_wide, zero_f), axis=1)
        local_grads = (
            jnp.einsum("fc,hc->fh", x_cols, first_bar, preferred_element_type=jnp.float32),
            jnp.einsum("ic,oc->io", first_act, second_bar, preferred_element_type=jnp.float32),
            jnp.einsum("hc,fc->hf", second_act, tend_bar, preferred_element_type=jnp.float32),
            jnp.stack([sea_part, land_part]),
        )
        a_zonal = field_bar[0]
        a_merid = field_bar[1]
        a_temp = field_bar[2]
        height_bar = lon_change(a_zonal, x_factor) + lat_change(a_merid)
        prefix, suffix, column_sum = vertical_sums(height_bar, a_temp)
        temp_bar = layer_thickness_fraction * prefix
        div_bar = (-suffix - surface_bar[None]) / NLEV
        zonal_bar = -lon_change(div_bar, x_factor) - sin_lat * a_merid
        merid_bar = -lat_change(div_bar) + sin_lat * a_zonal
        adj_fields = jnp.stack([zonal_bar, merid_bar, temp_bar])
        input_levels = to_levels(input_bar).astype(jnp.float32)
        field_bar = field_bar + TIME_STEP * adj_fields + input_levels
        surface_bar = surface_bar + TIME_STEP * column_sum
        summed = lax.psum(
            (local_grads[0], local_grads[1], local_grads[2], local_grads[3]), ("lev", "tile", "sec")
        )
        gradient = jax.tree.map(jnp.add, gradient, summed)
    return (
        current_fields_bundle,
        current_ground_pressure,
        field_bar,
        surface_bar,
        gradient[0],
        gradient[1],
        gradient[2],
        gradient[3],
    )


def solution(mesh):
    return jax.shard_map(
        on_device,
        mesh=mesh,
        in_specs=(
            P(None, ("lev", "sec"), None, "tile", None),
            P(None, "tile", None),
            P(None, ("lev", "sec"), None, "tile", None),
            P(None, "tile", None),
            P("tile", None),
            P(),
            P(),
            P(),
            P(),
        ),
        out_specs=(
            P(None, ("lev", "sec"), None, "tile", None),
            P(None, "tile", None),
            P(None, ("lev", "sec"), None, "tile", None),
            P(None, "tile", None),
            P(),
            P(),
            P(),
            P(),
        ),
        check_vma=False,
    )
```

profile of v0, /device:TPU:1, one launch (start us, length us, event | category | flops | bytes accessed | tf_op | source)
XLA Modules:
  0.0 1525.6 jit_solution(4728833632779786206)
XLA Ops:
  10.4 8.8 collective-permute-start
  19.2 1.9 collective-permute-start.1
  24.2 3.0 collective-permute-start.8
  27.2 2.6 collective-permute-start.9
  31.5 4.8 copy.305
  36.4 2.8 reshape.435
  39.1 13.2 all-to-all-start
  55.2 1.8 fusion.181
  58.4 1.8 fusion.173
  63.7 59.1 %all_gather.29 = f32[8,4,2,360]{3,1,2,0:T(4,128)} all-gather(f32[1,4,2,360]{3,1,2,0:T(4,128)S(1)} %copy.336), channel_id=1, replica_groups=mesh['lev'=4,'tile'=64,'sec'=2] {'lev','sec'}, dimensions={0}, use_global_device_ids=true | all-gather | bytes 103680 | tf_op jit(solution)/shard_map/all_gather | solution.py:33
  123.4 71.1 %all-reduce.2 = (f32[4,2,360]{2,1,0:T(2,128)}, f32[4,2,360]{2,1,0:T(2,128)}) all-reduce(f32[4,2,360]{2,1,0:T(2,128)S(1)} %get-tuple-element.428, f32[4,2,360]{2,1,0:T(2,128)S(1)} %get-tuple-element.453), channel_id=1, replica_groups=mesh['lev'=4,'tile'=64,'sec'=2] {'lev','sec'}, use_global_device_ids=true, to_apply=%region_1.2 | all-reduce | flops 5760 | bytes 46080 | tf_op jit(solution)/shard_map/psum | solution.py:72
  194.5 2.7 copy.380
  197.2 2.8 reshape.439
  200.0 57.2 %all_gather.25 = f32[8,4,2,360]{3,1,2,0:T(4,128)S(1)} all-gather(f32[1,4,2,360]{3,1,2,0:T(4,128)S(1)} %copy.295), channel_id=1, replica_groups=mesh['lev'=4,'tile'=64,'sec'=2] {'lev','sec'}, dimensions={0}, use_global_device_ids=true | all-gather | bytes 103680 | tf_op jit(solution)/shard_map/all_gather | solution.py:33
  259.3 56.7 %all_gather.24 = f32[8,4,2,360]{3,1,2,0:T(4,128)S(1)} all-gather(f32[1,4,2,360]{3,1,2,0:T(4,128)S(1)} %copy.294), channel_id=1, replica_groups=mesh['lev'=4,'tile'=64,'sec'=2] {'lev','sec'}, dimensions={0}, use_global_device_ids=true | all-gather | bytes 103680 | tf_op jit(solution)/shard_map/all_gather | solution.py:33
  321.2 57.2 %all_gather.28 = f32[8,4,2,360]{3,1,2,0:T(4,128)S(1)} all-gather(f32[1,4,2,360]{3,1,2,0:T(4,128)S(1)} %copy.335), channel_id=1, replica_groups=mesh['lev'=4,'tile'=64,'sec'=2] {'lev','sec'}, dimensions={0}, use_global_device_ids=true | all-gather | bytes 103680 | tf_op jit(solution)/shard_map/all_gather | solution.py:33
  380.6 33.9 %collective-permute-start.2 = (f32[8,4,1,360]{3,2,1,0:T(1,128)}, f32[8,4,1,360]{3,2,1,0:T(1,128)}, u32[]{:S(2)}, u32[]{:S(2)}) collective-permute-start(f32[8,4,1,360]{3,2,1,0:T(1,128)} %get-tuple-element.426), channel_id=1, source_target_pairs={{2,0},{4,2},{6,4},{8,6},{10,8},{12,10},{14,12},{16,14},{18,16},{20... | collective-permute-start | bytes 138248 | tf_op jit(solution)/shard_map/ppermute | solution.py:26
  414.5 2.5 collective-permute-start.3
  417.5 2.5 collective-permute-start.10
  420.0 3.1 collective-permute-start.11
  423.3 1.9 fusion.123
  425.2 7.0 all-to-all-start.4
  432.2 3.0 reshape.436
  435.2 2.2 copy.376
  437.5 3.2 fusion.23
  440.7 2.1 fusion.26
  444.0 2.8 all-to-all-done.4
  446.8 11.0 all-to-all-start.1
  462.2 3.0 reshape.440
  465.2 2.2 copy.382
  467.4 5.1 all-to-all-done.1
  473.5 1.8 fusion.156
  478.5 3.7 collective-permute-start.4
  482.3 3.1 collective-permute-start.5
  486.0 2.7 copy.377
  488.7 2.8 reshape.437
  491.5 7.5 all-to-all-start.2
  498.9 58.8 %all_gather.27 = f32[8,4,2,360]{3,1,2,0:T(4,128)S(1)} all-gather(f32[1,4,2,360]{3,1,2,0:T(4,128)S(1)} %copy.318), channel_id=1, replica_groups=mesh['lev'=4,'tile'=64,'sec'=2] {'lev','sec'}, dimensions={0}, use_global_device_ids=true | all-gather | bytes 103680 | tf_op jit(solution)/shard_map/all_gather | solution.py:33
  560.2 56.7 %all_gather.26 = f32[8,4,2,360]{3,1,2,0:T(4,128)S(1)} all-gather(f32[1,4,2,360]{3,1,2,0:T(4,128)S(1)} %copy.317), channel_id=1, replica_groups=mesh['lev'=4,'tile'=64,'sec'=2] {'lev','sec'}, dimensions={0}, use_global_device_ids=true | all-gather | bytes 103680 | tf_op jit(solution)/shard_map/all_gather | solution.py:33
  617.7 3.0 reshape.438
  622.1 2.1 fusion.29
  628.3 12.8 all-to-all-start.5
  644.3 11.3 all-to-all-done.5
  655.6 4.0 all-to-all-start.3
  663.3 15.9 %collective-permute-start.12 = (f32[8,4,1,360]{3,2,1,0:T(1,128)}, f32[8,4,1,360]{3,2,1,0:T(1,128)}, u32[]{:S(2)}, u32[]{:S(2)}) collective-permute-start(f32[8,4,1,360]{3,2,1,0:T(1,128)} %get-tuple-element.392), channel_id=1, source_target_pairs={{2,0},{4,2},{6,4},{8,6},{10,8},{12,10},{14,12},{16,14},{18,16},{20... | collective-permute-start | bytes 138248 | tf_op jit(solution)/shard_map/ppermute | solution.py:26
  679.2 4.8 collective-permute-start.13
  684.0 2.7 copy.383
  686.8 2.8 reshape.441
  691.7 14.2 all-to-all-start.6
  707.5 58.5 %all_gather.31 = f32[8,4,2,360]{3,1,2,0:T(4,128)S(1)} all-gather(f32[1,4,2,360]{3,1,2,0:T(4,128)S(1)} %copy.357), channel_id=1, replica_groups=mesh['lev'=4,'tile'=64,'sec'=2] {'lev','sec'}, dimensions={0}, use_global_device_ids=true | all-gather | bytes 103680 | tf_op jit(solution)/shard_map/all_gather | solution.py:33
  768.1 56.7 %all_gather.30 = f32[8,4,2,360]{3,1,2,0:T(4,128)S(1)} all-gather(f32[1,4,2,360]{3,1,2,0:T(4,128)S(1)} %copy.356), channel_id=1, replica_groups=mesh['lev'=4,'tile'=64,'sec'=2] {'lev','sec'}, dimensions={0}, use_global_device_ids=true | all-gather | bytes 103680 | tf_op jit(solution)/shard_map/all_gather | solution.py:33
  825.6 165.0 %all-reduce.8.cloned.1.call-done = (f32[4,2,360]{2,1,0:T(2,128)}, f32[4,2,360]{2,1,0:T(2,128)}, f32[4,2,360]{2,1,0:T(2,128)}, f32[4,2,360]{2,1,0:T(2,128)}, f32[4,2,360]{2,1,0:T(2,128)}, /*index=5*/f32[4,2,360]{2,1,0:T(2,128)}) async-done(((f32[4,2,360]{2,1,0:T(2,128)}, f32[4,2,360]{2,1,0:T(2,128)}, f32[4,2,360]{2,1,0:T(2,128)}, f32[4,2,360]{2,1,0:T(2,128)}, f32[4,2,360]{2,1,0:T(2,128)}, ...) | async-done | bytes 69136 | tf_op jit(solution)/shard_map/psum | solution.py:72
  996.7 7.3 collective-permute-start.14
  1003.9 3.3 collective-permute-start.15
  1007.2 1.9 collective-permute-start.6
  1009.2 3.6 collective-permute-start.7
  1016.1 3.0 reshape.442
  1019.1 2.2 copy.385
  1023.0 1.9 fusion.19
  1027.3 3.4 all-to-all-start.7
  1031.8 2.1 convolution_add_fusion
  1034.0 112.8 %psum.131 = f32[2,384]{1,0:T(2,128)} all-reduce(f32[2,384]{1,0:T(2,128)S(1)} %maximum_add_fusion.2), channel_id=1, replica_groups=mesh['lev'=4,'tile'=64,'sec'=2] {'lev','tile','sec'}, use_global_device_ids=true, to_apply=%region_32.33 | all-reduce | flops 768 | bytes 6144 | tf_op jit(solution)/shard_map/psum | solution.py:190
  1147.8 365.1 %all-reduce.6.cloned.1.call-done = (f32[192,384]{1,0:T(8,128)}, f32[384,384]{1,0:T(8,128)}, f32[384,192]{0,1:T(8,128)}) async-done(((f32[192,384]{1,0:T(8,128)}, f32[384,384]{1,0:T(8,128)}, f32[384,192]{0,1:T(8,128)}), (f32[192,384]{1,0:T(8,128)}, f32[384,384]{1,0:T(8,128)}, f32[384,192]{0,1:T(8,128)})) %all-reduce.6.cloned.1.call-update) | async-done | bytes 1179664 | tf_op jit(solution)/shard_map/psum | solution.py:190
  1514.5 1.9 copy.518
  (331 shorter events, 76.5 us)
Async XLA Ops:
  8.0 432.7 %copy-start = (bf16[384,384]{1,0:T(8,128)(2,1)S(1)}, bf16[384,384]{1,0:T(8,128)(2,1)}, u32[]{:S(2)}) copy-start(bf16[384,384]{1,0:T(8,128)(2,1)} %param.23) | copy-start | bytes 884740
  10.4 246.8 %collective-permute-start = (f32[8,4,1,360]{3,2,1,0:T(1,128)}, f32[8,4,1,360]{3,2,1,0:T(1,128)}, u32[]{:S(2)}, u32[]{:S(2)}) collective-permute-start(f32[8,4,1,360]{3,2,1,0:T(1,128)} %get-tuple-element.434), channel_id=1, source_target_pairs={{2,0},{4,2},{6,4},{8,6},{10,8},{12,10},{14,12},{16,14},{18,16},{20... | collective-permute-start | bytes 138248 | tf_op jit(solution)/shard_map/ppermute | solution.py:26
  19.2 238.0 %collective-permute-start.1 = (f32[8,4,1,360]{3,2,1,0:T(1,128)}, f32[8,4,1,360]{3,2,1,0:T(1,128)}, u32[]{:S(2)}, u32[]{:S(2)}) collective-permute-start(f32[8,4,1,360]{3,2,1,0:T(1,128)} %get-tuple-element.435), channel_id=1, source_target_pairs={{0,2},{2,4},{4,6},{6,8},{8,10},{10,12},{12,14},{14,16},{16,18},{18... | collective-permute-start | bytes 138248 | tf_op jit(solution)/shard_map/ppermute | solution.py:25
  24.2 295.1 %collective-permute-start.8 = (f32[8,4,1,360]{3,2,1,0:T(1,128)}, f32[8,4,1,360]{3,2,1,0:T(1,128)}, u32[]{:S(2)}, u32[]{:S(2)}) collective-permute-start(f32[8,4,1,360]{3,2,1,0:T(1,128)} %get-tuple-element.408), channel_id=1, source_target_pairs={{2,0},{4,2},{6,4},{8,6},{10,8},{12,10},{14,12},{16,14},{18,16},{20... | collective-permute-start | bytes 138248 | tf_op jit(solution)/shard_map/ppermute | solution.py:26
  27.2 292.1 %collective-permute-start.9 = (f32[8,4,1,360]{3,2,1,0:T(1,128)}, f32[8,4,1,360]{3,2,1,0:T(1,128)}, u32[]{:S(2)}, u32[]{:S(2)}) collective-permute-start(f32[8,4,1,360]{3,2,1,0:T(1,128)} %get-tuple-element.409), channel_id=1, source_target_pairs={{0,2},{2,4},{4,6},{6,8},{8,10},{10,12},{12,14},{14,16},{16,18},{18... | collective-permute-start | bytes 138248 | tf_op jit(solution)/shard_map/ppermute | solution.py:25
  31.5 21.5 %copy-start.1 = (f32[3,8,4,2,360]{4,3,2,1,0:T(2,128)S(1)}, f32[3,8,4,2,360]{4,3,2,1,0:T(2,128)}, u32[]{:S(2)}) copy-start(f32[3,8,4,2,360]{4,3,2,1,0:T(2,128)} %param.19) | copy-start | bytes 829444
  36.3 23.9 %copy-start.68 = (f32[2,384]{1,0:T(2,128)S(1)}, f32[2,384]{1,0:T(2,128)}, u32[]{:S(2)}) copy-start(f32[2,384]{1,0:T(2,128)} %param.25) | copy-start | bytes 9220
  36.4 24.5 %copy-start.69 = (s32[2,360]{1,0:T(2,128)S(1)}, s32[2,360]{1,0:T(2,128)}, u32[]{:S(2)}) copy-start(s32[2,360]{1,0:T(2,128)} %param.21) | copy-start | bytes 8644
  39.1 386.1 %all-to-all-start = ((bf16[8,2,4320]{2,1,0:T(2,128)(2,1)}), bf16[8,2,4320]{2,1,0:T(2,128)(2,1)}, u32[]{:S(2)}, u32[]{:S(2)}) async-start(bf16[8,2,4320]{2,1,0:T(2,128)(2,1)} %reshape.435), calls=%async_computation | async-start | bytes 278528 | tf_op jit(solution)/shard_map/all_to_all | solution.py:100
  62.0 132.4 %copy-start.40 = (f32[8,4,2,360]{3,2,1,0:T(2,128)}, f32[8,4,2,360]{3,2,1,0:T(2,128)S(1)}, u32[]{:S(2)}) copy-start(f32[8,4,2,360]{3,2,1,0:T(2,128)S(1)} %fusion.183) | copy-start | bytes 276484
  199.9 119.4 %copy-start.20 = (f32[8,4,2,360]{3,2,1,0:T(2,128)S(1)}, f32[8,4,2,360]{3,2,1,0:T(2,128)}, u32[]{:S(2)}) copy-start(f32[8,4,2,360]{3,2,1,0:T(2,128)} %copy-done.19) | copy-start | bytes 276484
  200.0 119.4 %copy-start.43 = (f32[8,4,2,359]{3,2,1,0:T(2,128)S(1)}, f32[8,4,2,359]{3,2,1,0:T(2,128)}, u32[]{:S(2)}) copy-start(f32[8,4,2,359]{3,2,1,0:T(2,128)} %get-tuple-element.406) | copy-start | bytes 275716
  200.0 119.4 %copy-start.44 = (f32[8,4,2,359]{3,2,1,0:T(2,128)S(1)}, f32[8,4,2,359]{3,2,1,0:T(2,128)}, u32[]{:S(2)}) copy-start(f32[8,4,2,359]{3,2,1,0:T(2,128)} %get-tuple-element.407) | copy-start | bytes 275716
  200.0 119.4 %copy-start.54 = (f32[8,4,2,1]{3,2,1,0:T(2,128)S(1)}, f32[8,4,2,1]{3,2,1,0:T(2,128)}, u32[]{:S(2)}) copy-start(f32[8,4,2,1]{3,2,1,0:T(2,128)} %get-tuple-element.404) | copy-start | bytes 772
  200.0 119.4 %copy-start.55 = (f32[8,4,2,1]{3,2,1,0:T(2,128)S(1)}, f32[8,4,2,1]{3,2,1,0:T(2,128)}, u32[]{:S(2)}) copy-start(f32[8,4,2,1]{3,2,1,0:T(2,128)} %get-tuple-element.405) | copy-start | bytes 772
  200.0 178.5 %copy-start.65 = (f32[8]{0:T(128)S(1)}, f32[8]{0:T(128)}, u32[]{:S(2)}) copy-start(f32[8]{0:T(128)} %copy-done.64) | copy-start | bytes 100
  200.0 179.2 %copy-start.39 = (f32[8,4,2,360]{3,2,1,0:T(2,128)S(1)}, f32[8,4,2,360]{3,2,1,0:T(2,128)}, u32[]{:S(2)}) copy-start(f32[8,4,2,360]{3,2,1,0:T(2,128)} %copy-done.38) | copy-start | bytes 276484
  200.0 179.2 %copy-start.63 = (f32[4,2,360]{2,1,0:T(2,128)S(1)}, f32[4,2,360]{2,1,0:T(2,128)}, u32[]{:S(2)}) copy-start(f32[4,2,360]{2,1,0:T(2,128)} %get-tuple-element.346) | copy-start | bytes 34564
  200.0 179.2 %copy-start.58 = (f32[4,2,360]{2,1,0:T(2,128)S(1)}, f32[4,2,360]{2,1,0:T(2,128)}, u32[]{:S(2)}) copy-start(f32[4,2,360]{2,1,0:T(2,128)} %param.20) | copy-start | bytes 34564
  257.2 166.1 %copy-start.61 = (f32[2]{0:T(128)S(1)}, f32[2]{0:T(128)}, u32[]{:S(2)}) copy-start(f32[2]{0:T(128)} %fusion.149) | copy-start | bytes 28
  379.3 45.9 %copy-start.7 = (f32[8,4,2,360]{3,2,1,0:T(2,128)}, f32[8,4,2,360]{3,2,1,0:T(2,128)S(1)}, u32[]{:S(2)}) copy-start(f32[8,4,2,360]{3,2,1,0:T(2,128)S(1)} %subtract_multiply_fusion.1) | copy-start | bytes 276484
  380.6 78.5 %collective-permute-start.2 = (f32[8,4,1,360]{3,2,1,0:T(1,128)}, f32[8,4,1,360]{3,2,1,0:T(1,128)}, u32[]{:S(2)}, u32[]{:S(2)}) collective-permute-start(f32[8,4,1,360]{3,2,1,0:T(1,128)} %get-tuple-element.426), channel_id=1, source_target_pairs={{2,0},{4,2},{6,4},{8,6},{10,8},{12,10},{14,12},{16,14},{18,16},{20... | collective-permute-start | bytes 138248 | tf_op jit(solution)/shard_map/ppermute | solution.py:26
  414.5 44.6 %collective-permute-start.3 = (f32[8,4,1,360]{3,2,1,0:T(1,128)}, f32[8,4,1,360]{3,2,1,0:T(1,128)}, u32[]{:S(2)}, u32[]{:S(2)}) collective-permute-start(f32[8,4,1,360]{3,2,1,0:T(1,128)} %get-tuple-element.427), channel_id=1, source_target_pairs={{0,2},{2,4},{4,6},{6,8},{8,10},{10,12},{12,14},{14,16},{16,18},{18... | collective-permute-start | bytes 138248 | tf_op jit(solution)/shard_map/ppermute | solution.py:25
  417.5 41.6 %collective-permute-start.10 = (f32[8,4,1,360]{3,2,1,0:T(1,128)}, f32[8,4,1,360]{3,2,1,0:T(1,128)}, u32[]{:S(2)}, u32[]{:S(2)}) collective-permute-start(f32[8,4,1,360]{3,2,1,0:T(1,128)} %get-tuple-element.398), channel_id=1, source_target_pairs={{2,0},{4,2},{6,4},{8,6},{10,8},{12,10},{14,12},{16,14},{18,16},{20... | collective-permute-start | bytes 138248 | tf_op jit(solution)/shard_map/ppermute | solution.py:26
  420.0 39.2 %collective-permute-start.11 = (f32[8,4,1,360]{3,2,1,0:T(1,128)}, f32[8,4,1,360]{3,2,1,0:T(1,128)}, u32[]{:S(2)}, u32[]{:S(2)}) collective-permute-start(f32[8,4,1,360]{3,2,1,0:T(1,128)} %get-tuple-element.399), channel_id=1, source_target_pairs={{0,2},{2,4},{4,6},{6,8},{8,10},{10,12},{12,14},{14,16},{16,18},{18... | collective-permute-start | bytes 138248 | tf_op jit(solution)/shard_map/ppermute | solution.py:25
  425.2 21.6 %all-to-all-start.4 = ((bf16[8,2,4320]{2,1,0:T(2,128)(2,1)}), bf16[8,2,4320]{2,1,0:T(2,128)(2,1)}, u32[]{:S(2)}, u32[]{:S(2)}) async-start(bf16[8,2,4320]{2,1,0:T(2,128)(2,1)} %reshape.439), calls=%async_computation.4 | async-start | bytes 278528 | tf_op jit(solution)/shard_map/all_to_all | solution.py:100
  440.7 17.2 %copy-start.45 = (f32[1,8,4,2,360]{4,3,2,1,0:T(2,128)S(1)}, f32[1,8,4,2,360]{4,3,2,1,0:T(2,128)}, u32[]{:S(2)}) copy-start(f32[1,8,4,2,360]{4,3,2,1,0:T(2,128)} %bitcast_add_fusion.3) | copy-start | bytes 276484
  440.7 17.8 %copy-start.50 = (f32[1,8,4,2,360]{4,3,2,1,0:T(2,128)S(1)}, f32[1,8,4,2,360]{4,3,2,1,0:T(2,128)}, u32[]{:S(2)}) copy-start(f32[1,8,4,2,360]{4,3,2,1,0:T(2,128)} %get-tuple-element.437) | copy-start | bytes 276484
  440.7 18.5 %copy-start.2 = (f32[3,8,4,2,360]{4,3,2,1,0:T(2,128)S(1)}, f32[3,8,4,2,360]{4,3,2,1,0:T(2,128)}, u32[]{:S(2)}) copy-start(f32[3,8,4,2,360]{4,3,2,1,0:T(2,128)} %param.17) | copy-start | bytes 829444
  440.7 18.5 %copy-start.6 = (f32[8,4,2,360]{3,2,1,0:T(2,128)S(1)}, f32[8,4,2,360]{3,2,1,0:T(2,128)}, u32[]{:S(2)}) copy-start(f32[8,4,2,360]{3,2,1,0:T(2,128)} %copy-done.5) | copy-start | bytes 276484
  440.7 18.5 %copy-start.8 = (f32[8,4,2,360]{3,2,1,0:T(2,128)S(1)}, f32[8,4,2,360]{3,2,1,0:T(2,128)}, u32[]{:S(2)}) copy-start(f32[8,4,2,360]{3,2,1,0:T(2,128)} %copy-done.7) | copy-start | bytes 276484
  440.7 20.5 %copy-start.46 = (f32[1,8,4,2,360]{4,3,2,1,0:T(2,128)S(1)}, f32[1,8,4,2,360]{4,3,2,1,0:T(2,128)}, u32[]{:S(2)}) copy-start(f32[1,8,4,2,360]{4,3,2,1,0:T(2,128)} %fusion.130) | copy-start | bytes 276484
  440.7 20.5 %copy-start.49 = (f32[1,8,4,2,360]{4,3,2,1,0:T(2,128)S(1)}, f32[1,8,4,2,360]{4,3,2,1,0:T(2,128)}, u32[]{:S(2)}) copy-start(f32[1,8,4,2,360]{4,3,2,1,0:T(2,128)} %get-tuple-element.436) | copy-start | bytes 276484
  442.9 18.3 %copy-start.13 = (bf16[384,360]{0,1:T(8,128)(2,1)}, bf16[384,360]{0,1:T(8,128)(2,1)S(1)}, u32[]{:S(2)}) copy-start(bf16[384,360]{0,1:T(8,128)(2,1)S(1)} %get-tuple-element.446) | copy-start | bytes 829444
  446.8 25.7 %all-to-all-start.1 = ((bf16[3,64,360]{2,0,1:T(4,128)(2,1)}), bf16[3,64,360]{2,0,1:T(4,128)(2,1)}, u32[]{:S(2)}, u32[]{:S(2)}) async-start(bf16[3,64,360]{2,0,1:T(4,128)(2,1)} %copy.308), calls=%async_computation.1 | async-start | bytes 393216 | tf_op jit(solution)/shard_map/all_to_all | solution.py:105
  478.5 79.1 %collective-permute-start.4 = (f32[8,4,1,360]{3,2,1,0:T(1,128)}, f32[8,4,1,360]{3,2,1,0:T(1,128)S(1)}, u32[]{:S(2)}, u32[]{:S(2)}) collective-permute-start(f32[8,4,1,360]{3,2,1,0:T(1,128)} %get-tuple-element.420), channel_id=1, source_target_pairs={{2,0},{4,2},{6,4},{8,6},{10,8},{12,10},{14,12},{16,14},{18,16},{20... | collective-permute-start | bytes 138248 | tf_op jit(solution)/shard_map/ppermute | solution.py:26
  482.3 75.4 %collective-permute-start.5 = (f32[8,4,1,360]{3,2,1,0:T(1,128)}, f32[8,4,1,360]{3,2,1,0:T(1,128)S(1)}, u32[]{:S(2)}, u32[]{:S(2)}) collective-permute-start(f32[8,4,1,360]{3,2,1,0:T(1,128)} %get-tuple-element.421), channel_id=1, source_target_pairs={{0,2},{2,4},{4,6},{6,8},{8,10},{10,12},{12,14},{14,16},{16,18},{18... | collective-permute-start | bytes 138248 | tf_op jit(solution)/shard_map/ppermute | solution.py:25
  491.5 126.3 %all-to-all-start.2 = ((bf16[8,2,4320]{2,1,0:T(2,128)(2,1)}), bf16[8,2,4320]{2,1,0:T(2,128)(2,1)}, u32[]{:S(2)}, u32[]{:S(2)}) async-start(bf16[8,2,4320]{2,1,0:T(2,128)(2,1)} %reshape.437), calls=%async_computation.2 | async-start | bytes 278528 | tf_op jit(solution)/shard_map/all_to_all | solution.py:100
  627.2 32.4 %copy-start.11 = (f32[3,8,4,2,360]{4,3,2,1,0:T(2,128)S(1)}, f32[3,8,4,2,360]{4,3,2,1,0:T(2,128)}, u32[]{:S(2)}) copy-start(f32[3,8,4,2,360]{4,3,2,1,0:T(2,128)} %fusion.81) | copy-start | bytes 829444
  628.3 27.3 %all-to-all-start.5 = ((bf16[3,64,360]{2,0,1:T(4,128)(2,1)}), bf16[3,64,360]{2,0,1:T(4,128)(2,1)S(1)}, u32[]{:S(2)}, u32[]{:S(2)}) async-start(bf16[3,64,360]{2,0,1:T(4,128)(2,1)} %copy.349), calls=%async_computation.5 | async-start | bytes 393216 | tf_op jit(solution)/shard_map/all_to_all | solution.py:105
  655.6 36.1 %all-to-all-start.3 = ((bf16[3,64,360]{2,0,1:T(4,128)(2,1)}), bf16[3,64,360]{2,0,1:T(4,128)(2,1)}, u32[]{:S(2)}, u32[]{:S(2)}) async-start(bf16[3,64,360]{2,0,1:T(4,128)(2,1)} %copy.333), calls=%async_computation.3 | async-start | bytes 393216 | tf_op jit(solution)/shard_map/all_to_all | solution.py:105
  663.3 102.7 %collective-permute-start.12 = (f32[8,4,1,360]{3,2,1,0:T(1,128)}, f32[8,4,1,360]{3,2,1,0:T(1,128)}, u32[]{:S(2)}, u32[]{:S(2)}) collective-permute-start(f32[8,4,1,360]{3,2,1,0:T(1,128)} %get-tuple-element.392), channel_id=1, source_target_pairs={{2,0},{4,2},{6,4},{8,6},{10,8},{12,10},{14,12},{16,14},{18,16},{20... | collective-permute-start | bytes 138248 | tf_op jit(solution)/shard_map/ppermute | solution.py:26
  679.2 86.8 %collective-permute-start.13 = (f32[8,4,1,360]{3,2,1,0:T(1,128)}, f32[8,4,1,360]{3,2,1,0:T(1,128)}, u32[]{:S(2)}, u32[]{:S(2)}) collective-permute-start(f32[8,4,1,360]{3,2,1,0:T(1,128)} %get-tuple-element.393), channel_id=1, source_target_pairs={{0,2},{2,4},{4,6},{6,8},{8,10},{10,12},{12,14},{14,16},{16,18},{18... | collective-permute-start | bytes 138248 | tf_op jit(solution)/shard_map/ppermute | solution.py:25
  689.5 135.3 %copy-start.67 = (f32[8]{0:T(128)S(1)}, f32[8]{0:T(128)}, u32[]{:S(2)}) copy-start(f32[8]{0:T(128)} %copy-done.64) | copy-start | bytes 100
  689.5 301.1 %copy-start.59 = (f32[4,2,360]{2,1,0:T(2,128)S(1)}, f32[4,2,360]{2,1,0:T(2,128)}, u32[]{:S(2)}) copy-start(f32[4,2,360]{2,1,0:T(2,128)} %param.20) | copy-start | bytes 34564
  689.5 303.4 %copy-start.37 = (f32[8,4,2,360]{3,2,1,0:T(2,128)S(1)}, f32[8,4,2,360]{3,2,1,0:T(2,128)}, u32[]{:S(2)}) copy-start(f32[8,4,2,360]{3,2,1,0:T(2,128)} %copy-done.36) | copy-start | bytes 276484
  689.5 304.1 %copy-start.60 = (f32[4,2,360]{2,1,0:T(2,128)S(1)}, f32[4,2,360]{2,1,0:T(2,128)}, u32[]{:S(2)}) copy-start(f32[4,2,360]{2,1,0:T(2,128)} %param.18) | copy-start | bytes 34564
  691.6 321.2 %copy-start.18 = (f32[1,8,4,2,360]{4,1,3,2,0:T(8,128)S(1)}, f32[1,8,4,2,360]{4,1,3,2,0:T(8,128)}, u32[]{:S(2)}) copy-start(f32[1,8,4,2,360]{4,1,3,2,0:T(8,128)} %copy-done.17) | copy-start | bytes 276484
  691.7 321.2 %copy-start.62 = (f32[2]{0:T(128)S(1)}, f32[2]{0:T(128)}, u32[]{:S(2)}) copy-start(f32[2]{0:T(128)} %fusion.149) | copy-start | bytes 28
  691.7 324.4 %all-to-all-start.6 = ((bf16[8,2,4320]{2,1,0:T(2,128)(2,1)}), bf16[8,2,4320]{2,1,0:T(2,128)(2,1)}, u32[]{:S(2)}, u32[]{:S(2)}) async-start(bf16[8,2,4320]{2,1,0:T(2,128)(2,1)} %reshape.441), calls=%async_computation.6 | async-start | bytes 278528 | tf_op jit(solution)/shard_map/all_to_all | solution.py:100
  705.8 284.8 %all-reduce.8.cloned.1.call-start = ((), (), s32[]{:S(2)}) async-start(), calls=%async_computation.9 | async-start | bytes 147456 | tf_op jit(solution)/shard_map/psum | solution.py:72
  706.8 306.4 %copy-start.4 = (f32[3,8,4,2,360]{4,1,3,2,0:T(8,128)S(1)}, f32[3,8,4,2,360]{4,1,3,2,0:T(8,128)}, u32[]{:S(2)}) copy-start(f32[3,8,4,2,360]{4,1,3,2,0:T(8,128)} %copy-done.3) | copy-start | bytes 829444
  766.0 248.0 %copy-start.24 = (f32[1,8,4,2,360]{4,1,3,2,0:T(8,128)S(1)}, f32[1,8,4,2,360]{4,1,3,2,0:T(8,128)}, u32[]{:S(2)}) copy-start(f32[1,8,4,2,360]{4,1,3,2,0:T(8,128)} %copy-done.23) | copy-start | bytes 276484
  766.0 248.0 %copy-start.26 = (f32[1,8,4,2,360]{4,1,3,2,0:T(8,128)S(1)}, f32[1,8,4,2,360]{4,1,3,2,0:T(8,128)}, u32[]{:S(2)}) copy-start(f32[1,8,4,2,360]{4,1,3,2,0:T(8,128)} %copy-done.25) | copy-start | bytes 276484
  824.8 190.3 %copy-start.41 = (f32[1,8,4,2,360]{4,1,3,2,0:T(8,128)S(1)}, f32[1,8,4,2,360]{4,1,3,2,0:T(8,128)}, u32[]{:S(2)}) copy-start(f32[1,8,4,2,360]{4,1,3,2,0:T(8,128)} %fusion.131) | copy-start | bytes 276484
  996.7 17.3 %collective-permute-start.14 = (f32[8,4,1,360]{3,2,1,0:T(1,128)S(1)}, f32[8,4,1,360]{3,2,1,0:T(1,128)S(1)}, u32[]{:S(2)}, u32[]{:S(2)}) collective-permute-start(f32[8,4,1,360]{3,2,1,0:T(1,128)S(1)} %get-tuple-element.378), channel_id=1, source_target_pairs={{2,0},{4,2},{6,4},{8,6},{10,8},{12,10},{14,12},{16,14},{18,16},{20... | collective-permute-start | bytes 138248 | tf_op jit(solution)/shard_map/ppermute | solution.py:26
  1003.9 10.0 collective-permute-start.15
  1007.2 6.7 collective-permute-start.6
  1009.2 4.8 collective-permute-start.7
  1025.5 121.3 %copy-start.42 = (f32[1,8,4,2,360]{4,1,3,2,0:T(8,128)S(1)}, f32[1,8,4,2,360]{4,1,3,2,0:T(8,128)}, u32[]{:S(2)}) copy-start(f32[1,8,4,2,360]{4,1,3,2,0:T(8,128)} %fusion.129) | copy-start | bytes 276484
  1025.5 121.3 %copy-start.47 = (f32[1,8,4,2,360]{4,1,3,2,0:T(8,128)S(1)}, f32[1,8,4,2,360]{4,1,3,2,0:T(8,128)}, u32[]{:S(2)}) copy-start(f32[1,8,4,2,360]{4,1,3,2,0:T(8,128)} %copy.365) | copy-start | bytes 276484
  1025.5 121.3 %copy-start.48 = (f32[1,8,4,2,360]{4,1,3,2,0:T(8,128)S(1)}, f32[1,8,4,2,360]{4,1,3,2,0:T(8,128)}, u32[]{:S(2)}) copy-start(f32[1,8,4,2,360]{4,1,3,2,0:T(8,128)} %copy.366) | copy-start | bytes 276484
  1027.3 119.5 %all-to-all-start.7 = ((bf16[3,64,360]{2,0,1:T(4,128)(2,1)}), bf16[3,64,360]{2,0,1:T(4,128)(2,1)S(1)}, u32[]{:S(2)}, u32[]{:S(2)}) async-start(bf16[3,64,360]{2,0,1:T(4,128)(2,1)} %copy.371), calls=%async_computation.7 | async-start | bytes 393216 | tf_op jit(solution)/shard_map/all_to_all | solution.py:105
  1030.7 482.1 %all-reduce.6.cloned.1.call-start = ((), (), s32[]{:S(2)}) async-start(), calls=%async_computation.8 | async-start | bytes 2359296 | tf_op jit(solution)/shard_map/psum | solution.py:190
  (35 other events, 117.6 us)
Sparse Core Ops, SparseCore 0:
  825.0 165.5 all-reduce.7
Sparse Core Ops, SparseCore 1:
  1038.4 474.4 all-reduce.5
where the time goes:
time: 1530 us
  blocking collectives  645 us (42%)
  waiting for transfers between devices  549 us (36%)
  starting transfers between devices  175 us (11%)
  local copies, waits for them, and re-layouts  88.4 us (6%)
  other arithmetic  30.4 us (2%)
  matrix products  20.7 us (1%)
  between operations  16.9 us (1%)
    all_gather x8, blocking collectives, carried_in(): gathered = jax.tree.map(lambda a: lax.all_gather(a, axis), part)  461 us
    psum x1, waiting for transfers between devices, on_device(): lax.psum((local_grads[0], local_grads[1], local_grads[2], local_grads[3])...  365 us
    psum x1, waiting for transfers between devices, vertical_sums(): lax.psum((rising_part, falling_part), ('lev', 'sec'))  165 us
    psum x1, blocking collectives, on_device(): lax.psum((local_grads[0], local_grads[1], local_grads[2], local_grads[3])...  113 us
    ppermute x8, starting transfers between devices, extended(): after = lax.ppermute(first, axis, down)  77 us
    psum x1, blocking collectives, vertical_sums(): lax.psum((rising_part, falling_part), ('lev', 'sec'))  71.1 us
    all_to_all x4, starting transfers between devices, to_columns(): lax.all_to_all(flattened, ('lev', 'sec'), split_axis=2, concat_axis=1, ti...  41.8 us
    unnamed x164, local copies, waits for them, and re-layouts  35 us
  transfers between devices with their start and end apart: 26, of which 5 were waited for; matrix products, arithmetic and copies ran while one was open for 7% of the time, Pallas kernels for 0%

commit v1 on v0

v1 whole, which is shorter than its diff:
```python
import math

import jax
import jax.numpy as jnp
from jax import lax
from jax.sharding import PartitionSpec as P

TIME_STEP = 0.1
COS_FLOOR = 0.2
INV_SQRT_TWO = 1.0 / math.sqrt(2.0)
INV_SQRT_TWO_PI = 1.0 / math.sqrt(2.0 * math.pi)
GROUP = ("lev", "sec")
EVERY = ("lev", "tile", "sec")
HIGH = lax.Precision.HIGHEST


def gelu_parts(values):
    cumulative = 0.5 * (1.0 + lax.erf(values * INV_SQRT_TWO))
    density = jnp.exp(-0.5 * values * values) * INV_SQRT_TWO_PI
    return (values * cumulative).astype(jnp.bfloat16), cumulative + values * density


def dot(a, b):
    return jnp.dot(a, b, preferred_element_type=jnp.float32)


def dot_t(a, b):
    return jnp.einsum("ac,bc->ab", a, b, preferred_element_type=jnp.float32)


def on_device(fields, surface, cot_fields, cot_surface, land_sea, w_in, w_mid, w_out, bias_in):
    nlev = 64
    tiles = lax.axis_size("tile")
    lev_i, tile_i, sec_i = (lax.axis_index(a) for a in EVERY)
    row_in_band = lax.rem(lev_i, 2)
    sample = lax.div(lev_i, 2) * 2 + sec_i
    row = tile_i * 2 + row_in_band
    rows = tiles * 2
    latitude = -0.5 * math.pi + (row.astype(jnp.float32) + 0.5) * (math.pi / rows)
    x_factor = 0.5 / jnp.maximum(jnp.cos(latitude), COS_FLOOR)
    sin_lat = jnp.sin(latitude)
    level = jnp.arange(nlev)
    weight = (1.0 / (level.astype(jnp.float32) + 1.0))[:, None]
    below = (level[:, None] >= level[None, :]).astype(jnp.float32)
    mask = land_sea[row_in_band] > 0
    bias_cols = jnp.where(mask[None, :], bias_in[1][:, None], bias_in[0][:, None])

    def device_of(r, bh, bl):
        return ((bh * 2 + r % 2) * tiles + r // 2) * 2 + bl

    up = [(device_of(r, h, l), device_of(r + 1, h, l)) for r in range(rows - 1) for h in (0, 1) for l in (0, 1)]
    down = [(j, i) for i, j in up]

    def halo(values):
        values = values.astype(jnp.bfloat16)
        before = lax.ppermute(values, EVERY, up).astype(jnp.float32)
        after = lax.ppermute(values, EVERY, down).astype(jnp.float32)
        return (after - before) * 0.5

    def dx(values):
        return (jnp.roll(values, -1, axis=-1) - jnp.roll(values, 1, axis=-1)) * x_factor

    def rising(values):
        return jnp.dot(below, values, precision=HIGH)

    def falling(values):
        return jnp.dot(below.T, values, precision=HIGH)

    def to_columns(values):
        split = values.reshape(3, 8, 2, 2, 2, 360)
        return split.transpose(2, 4, 3, 0, 1, 5).reshape(8, 24, 360).astype(jnp.bfloat16)

    sent = jnp.concatenate([to_columns(fields), to_columns(TIME_STEP * cot_fields)], axis=1)
    arrived = lax.all_to_all(sent, GROUP, split_axis=0, concat_axis=0, tiled=True)
    both = arrived.reshape(8, 2, 3, 8, 360).transpose(1, 2, 0, 3, 4)
    x0 = both[0].reshape(192, 360)
    t0 = both[1].reshape(192, 360)

    def mlp(x):
        first_act, first_slope = gelu_parts(dot(w_in.T, x) + bias_cols)
        second_act, second_slope = gelu_parts(dot(w_mid.T, first_act))
        tendency = dot(w_out.T, second_act).astype(jnp.bfloat16)
        return tendency, (first_act, first_slope, second_act, second_slope)

    def mlp_back(x, tend_bar, kept):
        first_act, first_slope, second_act, second_slope = kept
        second_bar = (dot(w_out, tend_bar) * second_slope).astype(jnp.bfloat16)
        first_bar = (dot(w_mid, second_bar) * first_slope).astype(jnp.bfloat16)
        input_bar = dot(w_in, first_bar).astype(jnp.bfloat16)
        wide = first_bar.astype(jnp.float32)
        zero = jnp.zeros((), jnp.float32)
        grads = (
            dot_t(x, first_bar),
            dot_t(first_act, second_bar),
            dot_t(second_act, tend_bar),
            jnp.stack([jnp.sum(jnp.where(mask, zero, wide), 1), jnp.sum(jnp.where(mask, wide, zero), 1)]),
        )
        return input_bar.astype(jnp.float32), grads

    def dynamics(state, surf, halos):
        u, v = state[:64], state[64:128]
        dv, dh = halos[:64], halos[64:]
        height = falling(weight * state[128:]) + surf
        div = dx(u) + dv
        flux = rising(div) / nlev
        change = jnp.concatenate([-dx(height) + sin_lat * v, -dh - sin_lat * u, -flux])
        return change, -jnp.sum(div, 0) / nlev

    def forward_halo(state, surf):
        return jnp.concatenate([state[64:128], falling(weight * state[128:]) + surf])

    def div_bar(bar, surf_bar):
        return (-falling(bar[128:]) - surf_bar) / nlev

    def backward_halo(bar, surf_bar):
        return jnp.concatenate([bar[64:128], div_bar(bar, surf_bar)])

    def adjoint(bar, surf_bar, halos):
        a_u, a_v = bar[:64], bar[64:128]
        hb = dx(a_u) + halos[:64]
        change = jnp.concatenate(
            [-dx(div_bar(bar, surf_bar)) - sin_lat * a_v, -halos[64:] + sin_lat * a_u, weight * rising(hb)]
        )
        return change, jnp.sum(hb, 0)

    def pick(values):
        return values[sample, row_in_band]

    state0, surf0 = x0.astype(jnp.float32), pick(surface)
    bar0, sbar0 = t0.astype(jnp.float32), TIME_STEP * pick(cot_surface)
    halos = halo(jnp.concatenate([forward_halo(state0, surf0), backward_halo(bar0, sbar0)]))
    tend0, kept0 = mlp(x0)
    dyn, dyn_surf = dynamics(state0, surf0, halos[:128])
    inc_a = TIME_STEP * (dyn + tend0.astype(jnp.float32))
    sinc_a = TIME_STEP * dyn_surf
    state1, surf1 = state0 + inc_a, surf0 + sinc_a
    x1 = state1.astype(jnp.bfloat16)
    halos1 = halo(forward_halo(state1, surf1))
    tend1, kept1 = mlp(x1)
    dyn, dyn_surf = dynamics(state1, surf1, halos1)
    inc = inc_a + TIME_STEP * (dyn + tend1.astype(jnp.float32))
    sinc = sinc_a + TIME_STEP * dyn_surf
    adj, adj_surf = adjoint(bar0, sbar0, halos[128:])
    input_bar, grads1 = mlp_back(x1, t0, kept1)
    ginc_a, gsinc_a = adj + input_bar, adj_surf
    bar1, sbar1 = bar0 + TIME_STEP * ginc_a, sbar0 + TIME_STEP * gsinc_a
    halos1 = halo(backward_halo(bar1, sbar1))
    input_bar, grads0 = mlp_back(x0, bar1.astype(jnp.bfloat16), kept0)
    adj, adj_surf = adjoint(bar1, sbar1, halos1)
    ginc, gsinc = ginc_a + adj + input_bar, gsinc_a + adj_surf

    def outgoing(change, surf_change):
        high = surf_change.astype(jnp.bfloat16)
        low = (surf_change - high.astype(jnp.float32)).astype(jnp.bfloat16)
        levels = change.astype(jnp.bfloat16).reshape(3, 8, 8, 360).transpose(1, 0, 2, 3).reshape(8, 24, 360)
        flat = jnp.broadcast_to(jnp.stack([high, low])[None], (8, 2, 360))
        return jnp.concatenate([levels, flat], axis=1)

    def returned(values):
        came = lax.all_to_all(values, GROUP, split_axis=0, concat_axis=0, tiled=True).astype(jnp.float32)
        levels = came[:, :24].reshape(2, 2, 2, 3, 8, 360).transpose(3, 4, 0, 2, 1, 5).reshape(3, 8, 4, 2, 360)
        flat = (came[:, 24] + came[:, 25]).reshape(2, 2, 2, 360).transpose(0, 2, 1, 3).reshape(4, 2, 360)
        return levels, flat

    df, ds = returned(outgoing(inc, sinc))
    dg, dgs = returned(outgoing(ginc, gsinc))

    total = jax.tree.map(jnp.add, grads0, grads1)
    shapes = [g.shape for g in total]
    packed = jnp.concatenate([g.reshape(-1) for g in total])
    count = packed.shape[0]
    packed = jnp.pad(packed, (0, 512 * 640 - count)).astype(jnp.bfloat16)

    def swap(values, axes):
        return lax.all_to_all(values, axes, split_axis=0, concat_axis=0, tiled=True)

    part = swap(packed.reshape(tiles, -1), "tile").astype(jnp.float32).sum(0).astype(jnp.bfloat16)
    part = swap(part.reshape(8, -1), GROUP).astype(jnp.float32).sum(0).astype(jnp.bfloat16)
    part = swap(jnp.broadcast_to(part[None], (8, part.shape[0])), GROUP).reshape(-1)
    full = swap(jnp.broadcast_to(part[None], (tiles, part.shape[0])), "tile").reshape(-1).astype(jnp.float32)
    outs, at = [], 0
    for s in shapes:
        size = s[0] * s[1]
        outs.append(full[at : at + size].reshape(s))
        at += size
    return (fields + df, surface + ds, cot_fields + dg, cot_surface + dgs, *outs)


def solution(mesh):
    levels = P(None, ("lev", "sec"), None, "tile", None)
    flat = P(None, "tile", None)
    return jax.shard_map(
        on_device,
        mesh=mesh,
        in_specs=(levels, flat, levels, flat, P("tile", None), P(), P(), P(), P()),
        out_specs=(levels, flat, levels, flat, P(), P(), P(), P()),
        check_vma=False,
    )
```

time: 1530 us -> 274 us (0.18)
  blocking collectives: 645 us -> 0 us
  waiting for transfers between devices: 549 us -> 129 us
  starting transfers between devices: 175 us -> 89.3 us
  local copies, waits for them, and re-layouts: 88.4 us -> 20 us
    psum x2 -> x0, waiting for transfers between devices: 530 us -> none  [the longest x1 365 us: on_device(): lax.psum((local_grads[0], local_grads[1], local_grads[2], local_grads[3])...]
    all_gather x8 -> x0, blocking collectives: 461 us -> none  [carried_in(): gathered = jax.tree.map(lambda a: lax.all_gather(a, axis), part)]
    psum x2 -> x0, blocking collectives: 184 us -> none  [the longest x1 113 us: on_device(): lax.psum((local_grads[0], local_grads[1], local_grads[2], local_grads[3])...]
    all_to_all x8 -> x7, waiting for transfers between devices: 19.3 us -> 123 us  [the longest x4 88.5 us: swap(): return lax.all_to_all(values, axes, split_axis=0, concat_axis=0, tiled=True)]
    ppermute x16 -> x6, starting transfers between devices: 102 us -> 18.2 us  [the longest x3 11.8 us: halo(): after = lax.ppermute(values, EVERY, down).astype(jnp.float32)]
    unnamed x164 -> x82, local copies, waits for them, and re-layouts: 35 us -> 9.15 us
    all_to_all x8 -> x7, starting transfers between devices: 73 us -> 71.1 us  [the longest x4 45.9 us: swap(): return lax.all_to_all(values, axes, split_axis=0, concat_axis=0, tiled=True)]
  transfers between devices with their start and end apart: 26 -> 13, of which waited for: 5 -> 9; matrix products, arithmetic and copies ran while one was open for 7% -> 13% of each run, Pallas kernels for 0% -> 0%
where the time goes in v1:
time: 274 us; the launch traced here: 273 us
  waiting for transfers between devices  129 us (47%)
  starting transfers between devices  89.3 us (33%)
  other arithmetic  23.4 us (9%)
  local copies, waits for them, and re-layouts  20 us (7%)
  matrix products  9.48 us (3%)
    all_to_all x4, waiting for transfers between devices, swap(): return lax.all_to_all(values, axes, split_axis=0, concat_axis=0, tiled=True)  88.5 us
    all_to_all x4, starting transfers between devices, swap(): return lax.all_to_all(values, axes, split_axis=0, concat_axis=0, tiled=True)  45.9 us
    all_to_all x2, waiting for transfers between devices, returned(): lax.all_to_all(values, GROUP, split_axis=0, concat_axis=0, tiled=True)  20.3 us
    all_to_all x1, starting transfers between devices, on_device(): lax.all_to_all(sent, GROUP, split_axis=0, concat_axis=0, tiled=True)  18.3 us
    all_to_all x1, waiting for transfers between devices, on_device(): lax.all_to_all(sent, GROUP, split_axis=0, concat_axis=0, tiled=True)  14.2 us
    ppermute x3, starting transfers between devices, halo(): after = lax.ppermute(values, EVERY, down).astype(jnp.float32)  11.8 us
    unnamed x82, local copies, waits for them, and re-layouts  9.15 us
    all_to_all x2, starting transfers between devices, returned(): lax.all_to_all(values, GROUP, split_axis=0, concat_axis=0, tiled=True)  7.01 us
  transfers between devices with their start and end apart: 13, of which 9 were waited for; matrix products, arithmetic and copies ran while one was open for 13% of the time, Pallas kernels for 0%

profile of v1, /device:TPU:1, one launch (start us, length us, event | category | flops | bytes accessed | tf_op | source)
XLA Modules:
  0.0 272.8 jit_solution(12728963192081036853)
XLA Ops:
  0.7 1.1 copy.69
  1.7 1.0 multiply_convert_fusion.4
  2.8 0.7 pad_maximum_fusion
  3.6 18.3 %all-to-all-start = ((bf16[8,48,360]{2,1,0:T(8,128)(2,1)}), bf16[8,48,360]{2,1,0:T(8,128)(2,1)S(1)}, u32[]{:S(2)}, u32[]{:S(2)}) async-start(bf16[8,48,360]{2,1,0:T(8,128)(2,1)} %pad_maximum_fusion), calls=%async_computation | async-start | bytes 589824 | tf_op jit(solution)/shard_map/all_to_all | solution.py:74
  22.0 0.7 dynamic-slice_reduce_fusion
  22.7 0.7 multiply_reduce_fusion
  23.6 14.2 %all-to-all-done = bf16[8,48,360]{2,1,0:T(8,128)(2,1)S(1)} async-done(((bf16[8,48,360]{2,1,0:T(8,128)(2,1)}), bf16[8,48,360]{2,1,0:T(8,128)(2,1)S(1)}, u32[]{:S(2)}, u32[]{:S(2)}) %all-to-all-start) | async-done | bytes 276512 | tf_op jit(solution)/shard_map/all_to_all | solution.py:74
  38.8 3.6 %collective-permute-start = (bf16[256,360]{1,0:T(8,128)(2,1)S(1)}, bf16[256,360]{1,0:T(8,128)(2,1)S(1)}, u32[]{:S(2)}, u32[]{:S(2)}) collective-permute-start(bf16[256,360]{1,0:T(8,128)(2,1)S(1)} %pad_maximum_fusion.1), channel_id=1, source_target_pairs={{128,0},{129,1},{384,256},{385,257},{2,128},{3,129},{258,384},{259... | collective-permute-start | bytes 552968 | tf_op jit(solution)/shard_map/ppermute | solution.py:57
  42.5 1.9 collective-permute-start.1
  45.6 1.5 collective-permute-done
  47.2 4.0 %collective-permute-done.1 = bf16[256,360]{1,0:T(8,128)(2,1)S(1)} collective-permute-done((bf16[256,360]{1,0:T(8,128)(2,1)S(1)}, bf16[256,360]{1,0:T(8,128)(2,1)S(1)}, u32[]{:S(2)}, u32[]{:S(2)}) %collective-permute-start.1) | collective-permute-done | bytes 184352 | tf_op jit(solution)/shard_map/ppermute | solution.py:56
  53.7 1.0 multiply_add_fusion
  55.3 0.6 pad_maximum_fusion.5
  55.9 4.5 %collective-permute-start.4 = (bf16[128,360]{1,0:T(8,128)(2,1)}, bf16[128,360]{1,0:T(8,128)(2,1)}, u32[]{:S(2)}, u32[]{:S(2)}) collective-permute-start(bf16[128,360]{1,0:T(8,128)(2,1)} %pad_maximum_fusion.5), channel_id=1, source_target_pairs={{128,0},{129,1},{384,256},{385,257},{2,128},{3,129},{258,384},{259... | collective-permute-start | bytes 276488 | tf_op jit(solution)/shard_map/ppermute | solution.py:57
  60.5 1.9 collective-permute-start.5
  62.4 0.7 fusion.110
  63.1 0.6 fusion.109
  63.8 0.7 fusion.100
  64.5 0.7 fusion.101
  65.5 0.7 pad_maximum_fusion.4
  66.1 3.6 %collective-permute-start.2 = (bf16[128,360]{1,0:T(8,128)(2,1)}, bf16[128,360]{1,0:T(8,128)(2,1)}, u32[]{:S(2)}, u32[]{:S(2)}) collective-permute-start(bf16[128,360]{1,0:T(8,128)(2,1)} %pad_maximum_fusion.4), channel_id=1, source_target_pairs={{128,0},{129,1},{384,256},{385,257},{2,128},{3,129},{258,384},{259... | collective-permute-start | bytes 276488 | tf_op jit(solution)/shard_map/ppermute | solution.py:57
  69.8 2.6 collective-permute-start.3
  73.1 0.6 fusion.45
  74.2 0.7 reshape.249
  74.9 1.4 fusion.10
  78.2 4.6 %reduce.19 = bf16[64,5120]{1,0:T(8,128)(2,1)S(1)} reduce(bf16[64,1,5120]{2,1,0:T(2,128)(2,1)S(1)} %all_to_all.38, bf16[]{:T(256)} %broadcast.213), dimensions={1}, to_apply=%all_to_all.38.reduce_sub_computation | reduce | bytes 1310722 | tf_op jit(solution)/shard_map/all_to_all | solution.py:175
  82.8 1.3 reshape.265
  84.1 19.8 %all-to-all-start.3 = ((bf16[64,2,2560]{2,1,0:T(2,128)(2,1)}), bf16[64,2,2560]{2,1,0:T(2,128)(2,1)S(1)}, u32[]{:S(2)}, u32[]{:S(2)}) async-start(bf16[64,2,2560]{2,1,0:T(2,128)(2,1)} %reshape.265), calls=%async_computation.3 | async-start | bytes 1310720 | tf_op jit(solution)/shard_map/all_to_all | solution.py:175
  104.3 1.0 subtract_multiply_fusion.1
  106.0 0.7 copy.70
  106.8 1.0 subtract_multiply_fusion.2
  107.8 0.7 fusion.74
  108.7 30.6 %all-to-all-done.3 = bf16[64,2,2560]{2,1,0:T(2,128)(2,1)S(1)} async-done(((bf16[64,2,2560]{2,1,0:T(2,128)(2,1)}), bf16[64,2,2560]{2,1,0:T(2,128)(2,1)S(1)}, u32[]{:S(2)}, u32[]{:S(2)}) %all-to-all-start.3) | async-done | bytes 655392 | tf_op jit(solution)/shard_map/all_to_all | solution.py:175
  139.3 0.5 reshape.266
  139.9 1.2 reduce_sum.104
  141.1 0.7 reduce.20
  141.8 0.7 reshape.267
  142.5 5.7 %all-to-all-start.4 = ((bf16[8,2,320]{2,1,0:T(2,128)(2,1)}), bf16[8,2,320]{2,1,0:T(2,128)(2,1)S(1)}, u32[]{:S(2)}, u32[]{:S(2)}) async-start(bf16[8,2,320]{2,1,0:T(2,128)(2,1)} %reshape.267), calls=%async_computation.4 | async-start | bytes 24576 | tf_op jit(solution)/shard_map/all_to_all | solution.py:175
  148.2 0.7 pad_maximum_fusion.3
  148.9 13.0 %all-to-all-done.4 = bf16[8,2,320]{2,1,0:T(2,128)(2,1)S(1)} async-done(((bf16[8,2,320]{2,1,0:T(2,128)(2,1)}), bf16[8,2,320]{2,1,0:T(2,128)(2,1)S(1)}, u32[]{:S(2)}, u32[]{:S(2)}) %all-to-all-start.4) | async-done | bytes 10272 | tf_op jit(solution)/shard_map/all_to_all | solution.py:175
  162.0 3.4 %all-to-all-start.2 = ((bf16[8,26,360]{2,1,0:T(8,128)(2,1)}), bf16[8,26,360]{2,1,0:T(8,128)(2,1)S(1)}, u32[]{:S(2)}, u32[]{:S(2)}) async-start(bf16[8,26,360]{2,1,0:T(8,128)(2,1)} %pad_maximum_fusion.3), calls=%async_computation.2 | async-start | bytes 393216 | tf_op jit(solution)/shard_map/all_to_all | solution.py:160
  165.9 0.7 reduce.21
  166.6 0.7 reshape.269
  167.3 12.5 %all-to-all-done.2 = bf16[8,26,360]{2,1,0:T(8,128)(2,1)S(1)} async-done(((bf16[8,26,360]{2,1,0:T(8,128)(2,1)}), bf16[8,26,360]{2,1,0:T(8,128)(2,1)S(1)}, u32[]{:S(2)}, u32[]{:S(2)}) %all-to-all-start.2) | async-done | bytes 149792 | tf_op jit(solution)/shard_map/all_to_all | solution.py:160
  179.9 3.3 %all-to-all-start.5 = ((bf16[8,2,320]{2,1,0:T(2,128)(2,1)}), bf16[8,2,320]{2,1,0:T(2,128)(2,1)S(1)}, u32[]{:S(2)}, u32[]{:S(2)}) async-start(bf16[8,2,320]{2,1,0:T(2,128)(2,1)} %reshape.269), calls=%async_computation.5 | async-start | bytes 24576 | tf_op jit(solution)/shard_map/all_to_all | solution.py:175
  183.2 0.7 pad_maximum_fusion.2
  183.9 13.0 %all-to-all-done.5 = bf16[8,2,320]{2,1,0:T(2,128)(2,1)S(1)} async-done(((bf16[8,2,320]{2,1,0:T(2,128)(2,1)}), bf16[8,2,320]{2,1,0:T(2,128)(2,1)S(1)}, u32[]{:S(2)}, u32[]{:S(2)}) %all-to-all-start.5) | async-done | bytes 10272 | tf_op jit(solution)/shard_map/all_to_all | solution.py:175
  196.9 3.6 %all-to-all-start.1 = ((bf16[8,26,360]{2,1,0:T(8,128)(2,1)}), bf16[8,26,360]{2,1,0:T(8,128)(2,1)S(1)}, u32[]{:S(2)}, u32[]{:S(2)}) async-start(bf16[8,26,360]{2,1,0:T(8,128)(2,1)} %pad_maximum_fusion.2), calls=%async_computation.1 | async-start | bytes 393216 | tf_op jit(solution)/shard_map/all_to_all | solution.py:160
  200.7 0.7 broadcast_in_dim.90
  201.4 4.6 %reduce.22 = bf16[64,5120]{1,0:T(8,128)(2,1)S(1)} reduce(bf16[64,1,5120]{2,1,0:T(2,128)(2,1)S(1)} %broadcast_in_dim.90, bf16[]{:T(256)} %broadcast.213), dimensions={1}, to_apply=%broadcast_in_dim.90.reduce_sub_computation | reduce | bytes 1310722 | tf_op jit(solution)/shard_map/broadcast_in_dim | solution.py:180
  206.0 1.3 reshape.271
  207.3 7.7 %all-to-all-done.1 = bf16[8,26,360]{2,1,0:T(8,128)(2,1)S(1)} async-done(((bf16[8,26,360]{2,1,0:T(8,128)(2,1)}), bf16[8,26,360]{2,1,0:T(8,128)(2,1)S(1)}, u32[]{:S(2)}, u32[]{:S(2)}) %all-to-all-start.1) | async-done | bytes 149792 | tf_op jit(solution)/shard_map/all_to_all | solution.py:160
  215.1 17.1 %all-to-all-start.6 = ((bf16[64,2,2560]{2,1,0:T(2,128)(2,1)}), bf16[64,2,2560]{2,1,0:T(2,128)(2,1)S(1)}, u32[]{:S(2)}, u32[]{:S(2)}) async-start(bf16[64,2,2560]{2,1,0:T(2,128)(2,1)} %reshape.271), calls=%async_computation.6 | async-start | bytes 1310720 | tf_op jit(solution)/shard_map/all_to_all | solution.py:175
  232.3 0.9 copy.59
  233.4 0.9 copy.58
  234.4 0.6 bitcast_add_fusion
  235.0 0.6 bitcast_add_fusion.1
  235.7 31.9 %all-to-all-done.6 = bf16[64,2,2560]{2,1,0:T(2,128)(2,1)S(1)} async-done(((bf16[64,2,2560]{2,1,0:T(2,128)(2,1)}), bf16[64,2,2560]{2,1,0:T(2,128)(2,1)S(1)}, u32[]{:S(2)}, u32[]{:S(2)}) %all-to-all-start.6) | async-done | bytes 655392 | tf_op jit(solution)/shard_map/all_to_all | solution.py:175
  267.5 0.5 reshape.272
  268.1 1.3 convert_element_type.295
  269.7 0.9 copy.60
  270.5 1.0 reshape.253
  271.5 0.8 reshape.252
  272.3 0.6 reshape.255
  (177 shorter events, 10.9 us)
Async XLA Ops:
  0.6 44.4 %copy-start = (bf16[384,384]{1,0:T(8,128)(2,1)S(1)}, bf16[384,384]{1,0:T(8,128)(2,1)}, u32[]{:S(2)}) copy-start(bf16[384,384]{1,0:T(8,128)(2,1)} %param.15) | copy-start | bytes 884740
  0.6 22.8 %copy-start.32 = (s32[2,360]{1,0:T(2,128)S(1)}, s32[2,360]{1,0:T(2,128)}, u32[]{:S(2)}) copy-start(s32[2,360]{1,0:T(2,128)} %param.13) | copy-start | bytes 8644
  0.7 22.9 %copy-start.31 = (f32[2,384]{1,0:T(2,128)S(1)}, f32[2,384]{1,0:T(2,128)}, u32[]{:S(2)}) copy-start(f32[2,384]{1,0:T(2,128)} %param.17) | copy-start | bytes 9220
  3.6 34.2 %all-to-all-start = ((bf16[8,48,360]{2,1,0:T(8,128)(2,1)}), bf16[8,48,360]{2,1,0:T(8,128)(2,1)S(1)}, u32[]{:S(2)}, u32[]{:S(2)}) async-start(bf16[8,48,360]{2,1,0:T(8,128)(2,1)} %pad_maximum_fusion), calls=%async_computation | async-start | bytes 589824 | tf_op jit(solution)/shard_map/all_to_all | solution.py:74
  23.5 28.4 %copy-start.33 = (pred[360]{0:T(512)(128)(4,1)}, pred[360]{0:T(512)(128)(4,1)S(1)}, u32[]{:S(2)}) copy-start(pred[360]{0:T(512)(128)(4,1)S(1)} %compare_reduce_fusion) | copy-start | bytes 1084
  23.5 29.2 %copy-start.28 = (f32[64]{0:T(128)}, f32[64]{0:T(128)S(1)}, u32[]{:S(2)}) copy-start(f32[64]{0:T(128)S(1)} %add_divide_fusion) | copy-start | bytes 772
  38.5 6.2 %copy-start.8 = (bf16[192,384]{1,0:T(8,128)(2,1)S(1)}, bf16[192,384]{1,0:T(8,128)(2,1)}, u32[]{:S(2)}) copy-start(bf16[192,384]{1,0:T(8,128)(2,1)} %param.14) | copy-start | bytes 442372
  38.8 8.3 %collective-permute-start = (bf16[256,360]{1,0:T(8,128)(2,1)S(1)}, bf16[256,360]{1,0:T(8,128)(2,1)S(1)}, u32[]{:S(2)}, u32[]{:S(2)}) collective-permute-start(bf16[256,360]{1,0:T(8,128)(2,1)S(1)} %pad_maximum_fusion.1), channel_id=1, source_target_pairs={{128,0},{129,1},{384,256},{385,257},{2,128},{3,129},{258,384},{259... | collective-permute-start | bytes 552968 | tf_op jit(solution)/shard_map/ppermute | solution.py:57
  42.5 8.7 %collective-permute-start.1 = (bf16[256,360]{1,0:T(8,128)(2,1)S(1)}, bf16[256,360]{1,0:T(8,128)(2,1)S(1)}, u32[]{:S(2)}, u32[]{:S(2)}) collective-permute-start(bf16[256,360]{1,0:T(8,128)(2,1)S(1)} %pad_maximum_fusion.1), channel_id=1, source_target_pairs={{0,128},{1,129},{256,384},{257,385},{128,2},{129,3},{384,258},{385... | collective-permute-start | bytes 552968 | tf_op jit(solution)/shard_map/ppermute | solution.py:56
  45.5 6.1 %copy-start.10 = (bf16[384,192]{0,1:T(8,128)(2,1)S(1)}, bf16[384,192]{0,1:T(8,128)(2,1)}, u32[]{:S(2)}) copy-start(bf16[384,192]{0,1:T(8,128)(2,1)} %param.16) | copy-start | bytes 442372
  51.4 3.6 %copy-start.22 = (f32[360]{0:T(512)}, f32[360]{0:T(512)S(1)}, u32[]{:S(2)}) copy-start(f32[360]{0:T(512)S(1)} %get-tuple-element.51) | copy-start | bytes 4324
  51.4 3.6 %copy-start.24 = (f32[360]{0:T(512)}, f32[360]{0:T(512)S(1)}, u32[]{:S(2)}) copy-start(f32[360]{0:T(512)S(1)} %get-tuple-element.42) | copy-start | bytes 4324
  52.3 1.4 copy-start.6
  53.3 19.5 %copy-start.18 = (bf16[384,360]{0,1:T(8,128)(2,1)}, bf16[384,360]{0,1:T(8,128)(2,1)S(1)}, u32[]{:S(2)}) copy-start(bf16[384,360]{0,1:T(8,128)(2,1)S(1)} %fusion.12) | copy-start | bytes 829444
  54.7 10.5 %copy-start.29 = (f32[64]{0:T(128)S(1)}, f32[64]{0:T(128)}, u32[]{:S(2)}) copy-start(f32[64]{0:T(128)} %copy-done.28) | copy-start | bytes 772
  55.9 48.4 %collective-permute-start.4 = (bf16[128,360]{1,0:T(8,128)(2,1)}, bf16[128,360]{1,0:T(8,128)(2,1)}, u32[]{:S(2)}, u32[]{:S(2)}) collective-permute-start(bf16[128,360]{1,0:T(8,128)(2,1)} %pad_maximum_fusion.5), channel_id=1, source_target_pairs={{128,0},{129,1},{384,256},{385,257},{2,128},{3,129},{258,384},{259... | collective-permute-start | bytes 276488 | tf_op jit(solution)/shard_map/ppermute | solution.py:57
  60.5 43.9 %collective-permute-start.5 = (bf16[128,360]{1,0:T(8,128)(2,1)}, bf16[128,360]{1,0:T(8,128)(2,1)}, u32[]{:S(2)}, u32[]{:S(2)}) collective-permute-start(bf16[128,360]{1,0:T(8,128)(2,1)} %pad_maximum_fusion.5), channel_id=1, source_target_pairs={{0,128},{1,129},{256,384},{257,385},{128,2},{129,3},{384,258},{385... | collective-permute-start | bytes 276488 | tf_op jit(solution)/shard_map/ppermute | solution.py:56
  66.1 40.6 %collective-permute-start.2 = (bf16[128,360]{1,0:T(8,128)(2,1)}, bf16[128,360]{1,0:T(8,128)(2,1)}, u32[]{:S(2)}, u32[]{:S(2)}) collective-permute-start(bf16[128,360]{1,0:T(8,128)(2,1)} %pad_maximum_fusion.4), channel_id=1, source_target_pairs={{128,0},{129,1},{384,256},{385,257},{2,128},{3,129},{258,384},{259... | collective-permute-start | bytes 276488 | tf_op jit(solution)/shard_map/ppermute | solution.py:57
  69.8 37.0 %collective-permute-start.3 = (bf16[128,360]{1,0:T(8,128)(2,1)}, bf16[128,360]{1,0:T(8,128)(2,1)}, u32[]{:S(2)}, u32[]{:S(2)}) collective-permute-start(bf16[128,360]{1,0:T(8,128)(2,1)} %pad_maximum_fusion.4), channel_id=1, source_target_pairs={{0,128},{1,129},{256,384},{257,385},{128,2},{129,3},{384,258},{385... | collective-permute-start | bytes 276488 | tf_op jit(solution)/shard_map/ppermute | solution.py:56
  72.3 0.8 copy-start.34
  73.7 2.6 copy-start.4
  76.4 0.9 copy-start.7
  84.1 21.2 %copy-start.14 = (f32[64,359]{1,0:T(8,128)S(1)}, f32[64,359]{1,0:T(8,128)}, u32[]{:S(2)}) copy-start(f32[64,359]{1,0:T(8,128)} %get-tuple-element.82) | copy-start | bytes 275716
  84.1 55.2 %all-to-all-start.3 = ((bf16[64,2,2560]{2,1,0:T(2,128)(2,1)}), bf16[64,2,2560]{2,1,0:T(2,128)(2,1)S(1)}, u32[]{:S(2)}, u32[]{:S(2)}) async-start(bf16[64,2,2560]{2,1,0:T(2,128)(2,1)} %reshape.265), calls=%async_computation.3 | async-start | bytes 1310720 | tf_op jit(solution)/shard_map/all_to_all | solution.py:175
  103.9 1.4 copy-start.15
  103.9 1.4 copy-start.16
  103.9 1.4 copy-start.17
  103.9 1.4 copy-start.19
  103.9 1.4 copy-start.20
  103.9 1.4 copy-start.21
  104.0 1.6 copy-start.30
  104.0 1.7 copy-start.3
  104.0 1.7 copy-start.5
  104.1 1.7 copy-start.9
  105.4 1.3 copy-start.25
  108.7 39.5 %copy-start.12 = (bf16[3,8,8,360]{3,2,0,1:T(8,128)(2,1)S(1)}, bf16[3,8,8,360]{3,2,0,1:T(8,128)(2,1)}, u32[]{:S(2)}) copy-start(bf16[3,8,8,360]{3,2,0,1:T(8,128)(2,1)} %copy.70) | copy-start | bytes 414724
  139.8 25.5 %copy-start.11 = (bf16[384,192]{0,1:T(8,128)(2,1)S(1)}, bf16[384,192]{0,1:T(8,128)(2,1)}, u32[]{:S(2)}) copy-start(bf16[384,192]{0,1:T(8,128)(2,1)} %param.16) | copy-start | bytes 442372
  139.9 25.5 %copy-start.13 = (f32[64,360]{1,0:T(8,128)S(1)}, f32[64,360]{1,0:T(8,128)}, u32[]{:S(2)}) copy-start(f32[64,360]{1,0:T(8,128)} %get-tuple-element.65) | copy-start | bytes 276484
  141.1 24.6 %copy-start.23 = (f32[360]{0:T(512)S(1)}, f32[360]{0:T(512)}, u32[]{:S(2)}) copy-start(f32[360]{0:T(512)} %copy-done.22) | copy-start | bytes 4324
  142.5 19.5 %all-to-all-start.4 = ((bf16[8,2,320]{2,1,0:T(2,128)(2,1)}), bf16[8,2,320]{2,1,0:T(2,128)(2,1)S(1)}, u32[]{:S(2)}, u32[]{:S(2)}) async-start(bf16[8,2,320]{2,1,0:T(2,128)(2,1)} %reshape.267), calls=%async_computation.4 | async-start | bytes 24576 | tf_op jit(solution)/shard_map/all_to_all | solution.py:175
  162.0 17.9 %all-to-all-start.2 = ((bf16[8,26,360]{2,1,0:T(8,128)(2,1)}), bf16[8,26,360]{2,1,0:T(8,128)(2,1)S(1)}, u32[]{:S(2)}, u32[]{:S(2)}) async-start(bf16[8,26,360]{2,1,0:T(8,128)(2,1)} %pad_maximum_fusion.3), calls=%async_computation.2 | async-start | bytes 393216 | tf_op jit(solution)/shard_map/all_to_all | solution.py:160
  179.9 17.0 %all-to-all-start.5 = ((bf16[8,2,320]{2,1,0:T(2,128)(2,1)}), bf16[8,2,320]{2,1,0:T(2,128)(2,1)S(1)}, u32[]{:S(2)}, u32[]{:S(2)}) async-start(bf16[8,2,320]{2,1,0:T(2,128)(2,1)} %reshape.269), calls=%async_computation.5 | async-start | bytes 24576 | tf_op jit(solution)/shard_map/all_to_all | solution.py:175
  196.9 18.1 %all-to-all-start.1 = ((bf16[8,26,360]{2,1,0:T(8,128)(2,1)}), bf16[8,26,360]{2,1,0:T(8,128)(2,1)S(1)}, u32[]{:S(2)}, u32[]{:S(2)}) async-start(bf16[8,26,360]{2,1,0:T(8,128)(2,1)} %pad_maximum_fusion.2), calls=%async_computation.1 | async-start | bytes 393216 | tf_op jit(solution)/shard_map/all_to_all | solution.py:160
  207.3 24.9 %copy-start.1 = (f32[3,8,4,2,360]{4,3,2,1,0:T(2,128)S(1)}, f32[3,8,4,2,360]{4,3,2,1,0:T(2,128)}, u32[]{:S(2)}) copy-start(f32[3,8,4,2,360]{4,3,2,1,0:T(2,128)} %param.11) | copy-start | bytes 829444
  215.1 52.5 %all-to-all-start.6 = ((bf16[64,2,2560]{2,1,0:T(2,128)(2,1)}), bf16[64,2,2560]{2,1,0:T(2,128)(2,1)S(1)}, u32[]{:S(2)}, u32[]{:S(2)}) async-start(bf16[64,2,2560]{2,1,0:T(2,128)(2,1)} %reshape.271), calls=%async_computation.6 | async-start | bytes 1310720 | tf_op jit(solution)/shard_map/all_to_all | solution.py:175
  232.3 1.1 copy-start.2
  233.3 1.1 copy-start.26
  233.3 1.7 copy-start.27

commit v2 on v1

v2 whole, which is shorter than its diff:
```python
import functools
import math

import jax
import jax.numpy as jnp
from jax import lax
from jax.experimental import pallas as pl
from jax.experimental.pallas import tpu as pltpu
from jax.sharding import PartitionSpec as P

TIME_STEP = 0.1
COS_FLOOR = 0.2
INV_SQRT_TWO = 1.0 / math.sqrt(2.0)
INV_SQRT_TWO_PI = 1.0 / math.sqrt(2.0 * math.pi)
EVERY = ("lev", "tile", "sec")
HIGH = lax.Precision.HIGHEST
MESH = pl.DeviceIdType.MESH
BF = jnp.bfloat16
F32 = jnp.float32
NLEV, NLON, LANES = 64, 360, 384
TILES, GROUP, PLANE, LINE = 64, 8, 32, 16
GROWS = 784
SHARE = 80


def dot(a, b):
    return jnp.dot(a, b, preferred_element_type=F32)


def dot_first(a, b):
    return lax.dot_general(a, b, (((0,), (0,)), ((), ())), preferred_element_type=F32)


def dot_last(a, b):
    return lax.dot_general(a, b, (((1,), (1,)), ((), ())), preferred_element_type=F32)


def kernel(
    sent_a, sent_b, flat, masks, bias, w_in, w_mid, w_out,
    out_f, out_g, g_in, g_mid, g_out,
    ra, rb, hs, hr, st, br, xs, a1, a2, s1, s2, inc, ginc, surf_ref,
    f_s, f_r, b_s, b_r, gacc, gs, gr, zs, zr, za, s80, ag,
    sems, hsem,
):
    lev, tile, sec = (lax.axis_index(a) for a in EVERY)
    r = lax.rem(lev, 2)
    me_g = lev * 2 + sec
    spot = lax.rem(tile, 8)
    z_lo = lax.div(tile, 8)
    me_p = lev * 8 + spot
    me_z = sec * 8 + z_lo

    def of_group(q):
        return (lax.div(q, 2), tile, lax.rem(q, 2))

    def of_plane(q):
        return (lax.div(q, 8), z_lo * 8 + lax.rem(q, 8), sec)

    def of_line(q):
        return (lev, lax.rem(q, 8) * 8 + spot, lax.div(q, 8))

    above = (lev + 1 - 2 * r, lax.rem(tile + r, TILES), sec)
    below_dev = (lev + 1 - 2 * r, lax.rem(tile + TILES - 1 + r, TILES), sec)

    barrier = pltpu.get_barrier_semaphore()

    def greet(where):
        pl.semaphore_signal(barrier, inc=1, device_id=where, device_id_type=MESH)

    def each(n, me, act):
        def go(p, c):
            act(lax.rem(me + p, n))
            return c

        lax.fori_loop(1, n, go, 0)

    each(GROUP, me_g, lambda q: greet(of_group(q)))
    greet(above)
    greet(below_dev)
    each(PLANE, me_p, lambda q: greet(of_plane(q)))
    each(LINE, me_z, lambda q: greet(of_line(q)))
    pl.semaphore_wait(barrier, GROUP - 1 + 2 + PLANE - 1 + LINE - 1)

    def push(src, dst, k, where):
        pltpu.make_async_remote_copy(
            src_ref=src, dst_ref=dst, send_sem=sems.at[2 * k], recv_sem=sems.at[2 * k + 1],
            device_id=where, device_id_type=MESH,
        ).start()

    def finish(ref, sem):
        pltpu.make_async_copy(ref, ref, sem).wait()

    each(GROUP, me_g, lambda q: push(sent_a.at[q], ra.at[me_g], 0, of_group(q)))
    each(GROUP, me_g, lambda q: push(sent_b.at[q], rb.at[me_g], 1, of_group(q)))

    lane = lax.broadcasted_iota(jnp.int32, (64, LANES), 1)
    real = lane < NLON
    level = lax.broadcasted_iota(jnp.int32, (64, LANES), 0).astype(F32)
    weight = 1.0 / (level + 1.0)
    row_i = lax.broadcasted_iota(jnp.int32, (64, 64), 0)
    col_i = lax.broadcasted_iota(jnp.int32, (64, 64), 1)
    tri_rise = jnp.where(row_i >= col_i, 1.0, 0.0).astype(F32)
    tri_fall = jnp.where(row_i <= col_i, 1.0, 0.0).astype(F32)
    x_factor, sin_lat = flat[3:4, :], flat[4:5, :]
    has_before, has_after = flat[5:6, :] > 0, flat[6:7, :] > 0
    land = flat[2:3, :] > 0

    def rising(values):
        return jnp.dot(tri_rise, values, precision=HIGH, preferred_element_type=F32)

    def falling(values):
        return jnp.dot(tri_fall, values, precision=HIGH, preferred_element_type=F32)

    def dx(values):
        rows = values.shape[0]
        ln = lax.broadcasted_iota(jnp.int32, (rows, LANES), 1)
        full = jnp.where(ln == NLON, pltpu.roll(values, NLON, 1), values)
        full = jnp.where(ln == LANES - 1, pltpu.roll(values, LANES - NLON, 1), full)
        return (pltpu.roll(full, LANES - 1, 1) - pltpu.roll(full, 1, 1)) * x_factor

    def halo_send(k, first, second):
        hs[k, 0:64, :] = first.astype(BF)
        hs[k, 64:128, :] = second.astype(BF)
        for way, where in ((0, above), (1, below_dev)):
            pltpu.make_async_remote_copy(
                src_ref=hs.at[k], dst_ref=hr.at[k, way], send_sem=hsem.at[k, way, 0],
                recv_sem=hsem.at[k, way, 1], device_id=where, device_id_type=MESH,
            ).start()

    def halo_take(k):
        for way in (0, 1):
            finish(hr.at[k, way], hsem.at[k, way, 1])
        before, after = hr[k, 0].astype(F32), hr[k, 1].astype(F32)
        zero = jnp.zeros((), F32)
        diff = (jnp.where(has_after, after, zero) - jnp.where(has_before, before, zero)) * 0.5
        return diff[0:64], diff[64:128]

    def forward(k):
        pre = dot_first(w_in[...], xs[k, 0:192, :]) + jnp.where(land, bias[:, 1:2], bias[:, 0:1])
        keep(pre, a1, s1, k)
        keep(dot_first(w_mid[...], a1[k]), a2, s2, k)
        return dot_first(w_out[...], a2[k]).astype(BF).astype(F32)

    def keep(pre, act, slope, k):
        cumulative = 0.5 * (1.0 + lax.erf(pre * INV_SQRT_TWO))
        density = jnp.exp(-0.5 * pre * pre) * INV_SQRT_TWO_PI
        act[k] = (pre * cumulative).astype(BF)
        slope[k] = cumulative + pre * density

    def backward(k, tend_bar):
        second_bar = (dot(w_out[...], tend_bar) * s2[k]).astype(BF)
        first_bar = (dot(w_mid[...], second_bar) * s1[k]).astype(BF)
        return second_bar, first_bar, dot(w_in[...], first_bar).astype(BF).astype(F32)

    def gradients(k, tend_bar, second_bar, first_bar):
        return (
            (0, dot_last(xs[k], first_bar)),
            (208, dot_last(a1[k], second_bar)),
            (592, dot_last(tend_bar, a2[k])),
        )

    def dynamics(surf, dv, dh):
        u, v, t = st[0:64, :], st[64:128, :], st[128:192, :]
        div = dx(u) + dv
        height = falling(weight * t) + surf
        flux = rising(div) * (1.0 / NLEV)
        return (
            -dx(height) + sin_lat * v, -dh - sin_lat * u, -flux,
            jnp.sum(div, axis=0, keepdims=True) * (-1.0 / NLEV),
        )

    def div_bar(surf_bar):
        return (-falling(br[128:192, :]) - surf_bar) * (1.0 / NLEV)

    def adjoint(surf_bar, da, ddb):
        a_u, a_v = br[0:64, :], br[64:128, :]
        hb = dx(a_u) + da
        return (
            -dx(div_bar(surf_bar)) - sin_lat * a_v, -ddb + sin_lat * a_u, weight * rising(hb),
            jnp.sum(hb, axis=0, keepdims=True),
        )

    def give(src, change, surf_change, dst, k):
        high = surf_change.astype(BF)
        low = (surf_change - high.astype(F32)).astype(BF)
        rows = lax.broadcasted_iota(jnp.int32, (8, LANES), 0)
        tail = jnp.where(rows == 0, high.astype(F32), jnp.where(rows == 1, low.astype(F32), 0.0))
        for g in range(GROUP):
            parts = [change[f * 64 + g * 8 : f * 64 + g * 8 + 8, :] for f in range(3)]
            src[g] = jnp.concatenate(parts + [tail], axis=0).astype(BF)
        dst[me_g] = src[me_g]
        each(GROUP, me_g, lambda q: push(src.at[q], dst.at[me_g], k, of_group(q)))

    xs[0, 192:208, :] = masks[...]
    xs[1, 192:208, :] = masks[...]
    ra[me_g] = sent_a[me_g]
    rb[me_g] = sent_b[me_g]
    surf0, sbar0 = flat[0:1, :], flat[1:2, :]

    finish(ra.at[pl.ds(0, 7)], sems.at[1])
    for g in range(GROUP):
        a = ra[g].astype(F32)
        for f in range(3):
            st[f * 64 + g * 8 : f * 64 + g * 8 + 8, :] = a[f * 8 : f * 8 + 8]
        br[g * 8 : g * 8 + 8, :] = a[24:32]
    halo_send(0, st[64:128, :], falling(weight * st[128:192, :]) + surf0)
    xs[0, 0:192, :] = st[...].astype(BF)
    tend = forward(0)

    finish(rb.at[pl.ds(0, 7)], sems.at[3])
    for g in range(GROUP):
        b = rb[g].astype(F32)
        br[64 + g * 8 : 72 + g * 8, :] = b[0:8]
        br[128 + g * 8 : 136 + g * 8, :] = b[8:16]
    halo_send(1, br[64:128, :], div_bar(sbar0))

    du, dv, dt, dsurf = dynamics(surf0, *halo_take(0))
    for i, d in enumerate((du, dv, dt)):
        at = slice(64 * i, 64 * i + 64)
        change = TIME_STEP * (d + tend[at])
        inc[at, :] = change
        st[at, :] = st[at, :] + change
    surf_inc = TIME_STEP * dsurf
    surf1 = surf0 + surf_inc
    halo_send(2, st[64:128, :], falling(weight * st[128:192, :]) + surf1)
    xs[1, 0:192, :] = st[...].astype(BF)
    tend = forward(1)

    t0 = br[...].astype(BF)
    second_bar, first_bar, input_bar = backward(1, t0)
    au, av, at_, asurf = adjoint(sbar0, *halo_take(1))
    for i, d in enumerate((au, av, at_)):
        at = slice(64 * i, 64 * i + 64)
        change = d + input_bar[at]
        ginc[at, :] = change
        br[at, :] = jnp.where(real, br[at, :] + TIME_STEP * change, 0.0)
    gsurf = asurf
    sbar1 = sbar0 + TIME_STEP * asurf
    halo_send(3, br[64:128, :], div_bar(sbar1))

    du, dv, dt, dsurf = dynamics(surf1, *halo_take(2))
    for i, d in enumerate((du, dv, dt)):
        at = slice(64 * i, 64 * i + 64)
        inc[at, :] = inc[at, :] + TIME_STEP * (d + tend[at])
    give(f_s, inc, surf_inc + TIME_STEP * dsurf, f_r, 2)

    for at, g in gradients(1, t0, second_bar, first_bar):
        gacc[at : at + g.shape[0], :] = g

    t1 = br[...].astype(BF)
    second_bar, first_bar, input_bar = backward(0, t1)
    gs[3 * GROWS :, :] = jnp.zeros((PLANE * SHARE - 3 * GROWS, 128), BF)
    for at, g in gradients(0, t1, second_bar, first_bar):
        total = (gacc[at : at + g.shape[0], :] + g).astype(BF)
        for b in range(3):
            gs[GROWS * b + at : GROWS * b + at + g.shape[0], :] = total[:, 128 * b : 128 * b + 128]

    def share(ref, q):
        return ref.at[pl.ds(pl.multiple_of(q * SHARE, 16), SHARE)]

    each(PLANE, me_p, lambda q: push(share(gs, q), gr.at[me_p], 3, of_plane(q)))

    au, av, at_, asurf = adjoint(sbar1, *halo_take(3))
    for i, d in enumerate((au, av, at_)):
        at = slice(64 * i, 64 * i + 64)
        ginc[at, :] = ginc[at, :] + d + input_bar[at]
    give(b_s, ginc, gsurf + asurf, b_r, 4)

    finish(gr.at[pl.ds(0, PLANE - 1)], sems.at[7])
    mine = gs[pl.ds(pl.multiple_of(me_p * SHARE, 16), SHARE), :].astype(F32)
    s80[...] = lax.fori_loop(
        1, PLANE, lambda p, acc: acc + gr[lax.rem(me_p + p, PLANE)].astype(F32), mine
    )
    for k in range(LINE):
        zs[k, 0:5, :] = s80[5 * k : 5 * k + 5, :]
        zs[k, 5:8, :] = jnp.zeros((3, 128), F32)
    each(LINE, me_z, lambda q: push(zs.at[q], zr.at[me_z], 5, of_line(q)))
    finish(zr.at[pl.ds(0, LINE - 1)], sems.at[11])
    za[me_z] = lax.fori_loop(
        1, LINE, lambda p, acc: acc + zr[lax.rem(me_z + p, LINE)], zs[me_z]
    )
    each(LINE, me_z, lambda q: push(za.at[me_z], za.at[me_z], 6, of_line(q)))
    finish(za.at[pl.ds(0, LINE - 1)], sems.at[13])
    for k in range(LINE):
        s80[5 * k : 5 * k + 5, :] = za[k, 0:5, :]
    ag[pl.ds(pl.multiple_of(me_p * SHARE, 16), SHARE), :] = s80[...].astype(BF)
    each(PLANE, me_p, lambda q: push(share(ag, me_p), share(ag, me_p), 7, of_plane(q)))

    finish(f_r.at[pl.ds(0, 7)], sems.at[5])
    out_f[...] = f_r[...]
    finish(b_r.at[pl.ds(0, 7)], sems.at[9])
    out_g[...] = b_r[...]
    finish(ag.at[pl.ds(0, (PLANE - 1) * SHARE)], sems.at[15])
    for b in range(3):
        lanes = slice(128 * b, 128 * b + 128)
        base = GROWS * b
        g_in[:, lanes] = ag[base : base + 208, :].astype(F32)
        g_mid[:, lanes] = ag[base + 208 : base + 592, :].astype(F32)
        g_out[:, lanes] = ag[base + 592 : base + 784, :].astype(F32)

    finish(ra.at[pl.ds(0, 7)], sems.at[0])
    finish(rb.at[pl.ds(0, 7)], sems.at[2])
    finish(f_s.at[pl.ds(0, 7)], sems.at[4])
    finish(gr.at[pl.ds(0, PLANE - 1)], sems.at[6])
    finish(b_s.at[pl.ds(0, 7)], sems.at[8])
    finish(zs.at[pl.ds(0, LINE - 1)], sems.at[10])
    finish(zs.at[pl.ds(0, LINE - 1)], sems.at[12])
    finish(ag.at[pl.ds(0, (PLANE - 1) * SHARE)], sems.at[14])
    for k in range(4):
        for way in (0, 1):
            finish(hs.at[k], hsem.at[k, way, 0])


def call(*operands):
    def v(shape, dtype):
        return pltpu.VMEM(shape, dtype)

    slab = (GROUP, 32, LANES)
    hidden = (2, 384, LANES)
    return pl.pallas_call(
        kernel,
        out_shape=(
            jax.ShapeDtypeStruct(slab, BF),
            jax.ShapeDtypeStruct(slab, BF),
            jax.ShapeDtypeStruct((208, 384), F32),
            jax.ShapeDtypeStruct((384, 384), F32),
            jax.ShapeDtypeStruct((192, 384), F32),
        ),
        in_specs=[pl.BlockSpec(memory_space=pltpu.VMEM)] * 8,
        out_specs=tuple([pl.BlockSpec(memory_space=pltpu.VMEM)] * 5),
        scratch_shapes=[
            v(slab, BF), v((GROUP, 16, LANES), BF),
            v((4, 128, LANES), BF), v((4, 2, 128, LANES), BF),
            v((192, LANES), F32), v((192, LANES), F32), v((2, 208, LANES), BF),
            v(hidden, BF), v(hidden, BF), v(hidden, F32), v(hidden, F32),
            v((192, LANES), F32), v((192, LANES), F32), v((8, LANES), F32),
            v(slab, BF), v(slab, BF), v(slab, BF), v(slab, BF),
            v((GROWS, 384), F32), v((PLANE * SHARE, 128), BF), v((PLANE, SHARE, 128), BF),
            v((LINE, 8, 128), F32), v((LINE, 8, 128), F32), v((LINE, 8, 128), F32),
            v((SHARE, 128), F32), v((PLANE * SHARE, 128), BF),
            pltpu.SemaphoreType.DMA((16,)), pltpu.SemaphoreType.DMA((4, 2, 2)),
        ],
        compiler_params=pltpu.CompilerParams(
            collective_id=0, has_side_effects=True, vmem_limit_bytes=40 * 2**20
        ),
        name="window",
    )(*operands)


def on_device(fields, surface, cot_fields, cot_surface, land_sea, w_in, w_mid, w_out, bias_in):
    lev_i, tile_i, sec_i = (lax.axis_index(a) for a in EVERY)
    row_in_band = lax.rem(lev_i, 2)
    sample = lax.div(lev_i, 2) * 2 + sec_i
    row = tile_i * 2 + row_in_band
    latitude = -0.5 * math.pi + (row.astype(F32) + 0.5) * (math.pi / (2 * TILES))
    x_factor = 0.5 / jnp.maximum(jnp.cos(latitude), COS_FLOOR)
    sin_lat = jnp.sin(latitude)

    def pad(values):
        return jnp.pad(values, [(0, 0)] * (values.ndim - 1) + [(0, LANES - NLON)])

    def to_columns(values):
        split = values.astype(BF).reshape(3, 8, 2, 2, 2, NLON)
        return pad(split.transpose(2, 4, 3, 0, 1, 5).reshape(8, 24, NLON))

    sent = jnp.concatenate([to_columns(fields), to_columns(TIME_STEP * cot_fields)], axis=1)
    mask = land_sea[row_in_band] > 0

    def line(value):
        return jnp.broadcast_to(value, (NLON,)).astype(F32)

    flat = pad(
        jnp.stack(
            [
                surface[sample, row_in_band],
                TIME_STEP * cot_surface[sample, row_in_band],
                mask.astype(F32),
            ]
        )
    )
    consts = jnp.stack([x_factor, sin_lat, (row > 0).astype(F32), (row < 2 * TILES - 1).astype(F32), 0.0 * x_factor])
    flat = jnp.concatenate([flat, jnp.broadcast_to(consts[:, None], (5, LANES))])
    masks = jnp.pad(jnp.stack([~mask, mask]).astype(BF), ((0, 14), (0, LANES - NLON)))
    came_f, came_g, g_in, g_mid, g_out = call(
        sent[:, :32], sent[:, 32:], flat, masks, bias_in.T, w_in, w_mid, w_out
    )

    def returned(came):
        came = came[:, :, :NLON].astype(F32)
        levels = came[:, :24].reshape(2, 2, 2, 3, 8, NLON).transpose(3, 4, 0, 2, 1, 5).reshape(3, 8, 4, 2, NLON)
        level_flat = (came[:, 24] + came[:, 25]).reshape(2, 2, 2, NLON).transpose(0, 2, 1, 3).reshape(4, 2, NLON)
        return levels, level_flat

    df, ds = returned(came_f)
    dg, dgs = returned(came_g)
    return (
        fields + df,
        surface + ds,
        cot_fields + dg,
        cot_surface + dgs,
        g_in[:192],
        g_mid,
        g_out.T,
        g_in[192:194],
    )


def solution(mesh):
    levels = P(None, ("lev", "sec"), None, "tile", None)
    flat = P(None, "tile", None)
    return jax.shard_map(
        on_device,
        mesh=mesh,
        in_specs=(levels, flat, levels, flat, P("tile", None), P(), P(), P(), P()),
        out_specs=(levels, flat, levels, flat, P(), P(), P(), P()),
        check_vma=False,
    )
```

time: 274 us -> 105 us (0.38)
  waiting for transfers between devices: 129 us -> 0 us
  Pallas kernels: 0 us -> 91.5 us
  starting transfers between devices: 89.3 us -> 0 us
  other arithmetic: 23.4 us -> 4.54 us
  local copies, waits for them, and re-layouts: 20 us -> 7.96 us
  matrix products: 9.48 us -> 0 us
    all_to_all x7 -> x0, waiting for transfers between devices: 123 us -> none  [the longest x4 88.5 us: swap(): return lax.all_to_all(values, axes, split_axis=0, concat_axis=0, tiled=True)]
    pallas_call x0 -> x1, Pallas kernels: none -> 91.5 us  [call(): pl.pallas_call(kernel, out_shape=(jax.ShapeDtypeStruct(slab, BF), jax.Sha...]
    all_to_all x7 -> x0, starting transfers between devices: 71.1 us -> none  [the longest x4 45.9 us: swap(): return lax.all_to_all(values, axes, split_axis=0, concat_axis=0, tiled=True)]
    ppermute x6 -> x0, starting transfers between devices: 18.2 us -> none  [the longest x3 11.8 us: halo(): after = lax.ppermute(values, EVERY, down).astype(jnp.float32)]
    dot_general x26 -> x0, matrix products: 9.48 us -> none  [the longest x12 4.95 us: dot(): return jnp.dot(a, b, preferred_element_type=jnp.float32)]
    ppermute x6 -> x0, waiting for transfers between devices: 5.59 us -> none  [the longest x3 4.05 us: halo(): before = lax.ppermute(values, EVERY, up).astype(jnp.float32)]
    all_to_all x3 -> x0, other arithmetic: 5.34 us -> none  [swap(): return lax.all_to_all(values, axes, split_axis=0, concat_axis=0, tiled=True)]
    broadcast_in_dim x2 -> x0, other arithmetic: 5.28 us -> none  [the longest x1 4.57 us: on_device(): jnp.broadcast_to(part[None], (tiles, part.shape[0]))]
  transfers between devices with their start and end apart: 13 -> 0, of which waited for: 9 -> 0; matrix products, arithmetic and copies ran while one was open for 13% -> 0% of each run, Pallas kernels for 0% -> 0%
where the time goes in v2:
time: 105 us
  Pallas kernels  91.5 us (87%)
  local copies, waits for them, and re-layouts  7.96 us (8%)
  other arithmetic  4.54 us (4%)
  between operations  1.09 us (1%)
    pallas_call x1, Pallas kernels, call(): pl.pallas_call(kernel, out_shape=(jax.ShapeDtypeStruct(slab, BF), jax.Sha...  91.5 us
    unnamed x22, local copies, waits for them, and re-layouts  6.01 us

profile of v2, /device:TPU:1, one launch (start us, length us, event | category | flops | bytes accessed | tf_op | source)
XLA Modules:
  0.0 105.1 jit_solution(7472279365451215076)
XLA Ops:
  0.8 0.0 copy-start.5
  0.9 0.0 copy-start.6
  0.9 0.1 stack.42
  1.0 0.1 pad.25.clone
  1.0 0.5 copy-done.5
  1.6 0.0 copy-done.6
  1.6 0.0 copy-start.8
  1.6 0.7 copy-done.8
  2.3 0.1 pad_maximum_fusion.flat
  2.4 0.0 copy-start.3
  2.4 1.1 %convert_element_type.29 = bf16[3,8,4,2,360]{4,3,2,1,0:T(2,128)(2,1)S(1)} convert(f32[3,8,4,2,360]{4,3,2,1,0:T(2,128)} %param.9) | non-fusion elementwise | flops 69120 | bytes 414720 | tf_op jit(solution)/shard_map/convert_element_type | solution.py:363
  3.6 0.0 copy-done.3
  3.6 0.2 multiply_convert_fusion
  3.8 0.0 copy-start.4
  3.8 0.9 copy-done.4
  4.7 0.0 copy-start.7
  4.7 0.0 copy-start
  4.7 0.1 copy.20.w_out
  4.9 0.5 copy-done.7
  5.4 0.0 copy-start.1
  5.4 0.1 copy.19
  5.5 0.1 copy-done
  5.7 0.6 copy-done.1
  6.3 91.5 %window.1 = (bf16[8,32,384]{2,1,0:T(8,128)(2,1)S(1)}, bf16[8,32,384]{2,1,0:T(8,128)(2,1)S(1)}, f32[208,384]{1,0:T(8,128)S(1)}, f32[384,384]{1,0:T(8,128)S(1)}, f32[192,384]{1,0:T(8,128)S(1)}) custom-call(bf16[8,32,384]{2,1,0:T(8,128)(2,1)S(1)} %fusion.1.sent_a, bf16[8,16,384]{2,1,0:T(8,128)(2,1)S(1)} %pad_slice_fusion.sent_b, ...), custom_call_target="tpu_custom_call" | custom-call | tf_op jit(solution)/shard_map/window/pallas_call | solution.py:320
  97.8 0.6 slice.47
  98.4 0.7 slice.46
  99.2 0.0 copy-start.2
  99.3 0.2 copy.21
  99.4 0.8 copy-done.2
  100.2 0.9 add.55
  101.1 0.6 bitcast_add_fusion.1
  101.8 0.2 copy.23
  102.0 0.9 add.59
  102.9 0.6 bitcast_add_fusion
  103.5 0.8 copy.29
  104.3 0.7 copy.30
  (21 shorter events, 0.4 us)
Async XLA Ops:
  0.8 0.7 copy-start.5
  0.9 0.7 copy-start.6
  1.6 0.7 copy-start.8
  2.4 1.1 %copy-start.3 = (f32[3,8,4,2,360]{4,3,2,1,0:T(2,128)S(1)}, f32[3,8,4,2,360]{4,3,2,1,0:T(2,128)}, u32[]{:S(2)}) copy-start(f32[3,8,4,2,360]{4,3,2,1,0:T(2,128)} %param.11) | copy-start | bytes 829444
  3.8 0.9 copy-start.4
  4.7 0.7 copy-start.7
  4.7 1.0 copy-start
  5.4 0.9 copy-start.1
  99.2 1.0 copy-start.2

commit v3 on v2

v3 whole, which is shorter than its diff:
```python
import functools
import math

import jax
import jax.numpy as jnp
from jax import lax
from jax.experimental import pallas as pl
from jax.experimental.pallas import tpu as pltpu
from jax.sharding import PartitionSpec as P

TIME_STEP = 0.1
COS_FLOOR = 0.2
INV_SQRT_TWO = 1.0 / math.sqrt(2.0)
INV_SQRT_TWO_PI = 1.0 / math.sqrt(2.0 * math.pi)
EVERY = ("lev", "tile", "sec")
HIGH = lax.Precision.HIGHEST
MESH = pl.DeviceIdType.MESH
BF = jnp.bfloat16
F32 = jnp.float32
NLEV, NLON, LANES = 64, 360, 384
TILES, GROUP, PLANE = 64, 8, 32
GROWS = 784
PART = (512, 272)
SHARE = (48, 32)
SLAB = (16, 640)


def dot(a, b):
    return jnp.dot(a, b, preferred_element_type=F32)


def dot_last(a, b):
    return lax.dot_general(a, b, (((1,), (1,)), ((), ())), preferred_element_type=F32)


def kernel(
    sent, consts, surface, cot_surface, land_sea, bias, w_in_h, w_mid_h, w_out_h,
    out_f, out_g, g_in, g_mid, g_out, g_bias,
    w_in, w_mid, w_out, w_in_t, w_mid_t, w_out_t, sv, cv, mv, bv, flat, bmat,
    a_s, b_s, ra, rb, hs, hr, st, br, xs, a1, a2, s1, s2, inc, ginc,
    f_s, f_r, o_s, o_r, gacc, gs0, gs1, gr0, gr1, near0, near1, far0, far1, ag0, ag1,
    sems, hsem, wsem,
):
    lev, tile, sec = (lax.axis_index(a) for a in EVERY)
    r = lax.rem(lev, 2)
    me_g = lev * 2 + sec
    spot = lax.rem(tile, 8)
    z_lo = lax.div(tile, 8)
    me_p = lev * 8 + spot
    pos = lax.rem(z_lo, 4)
    quad = lax.div(z_lo, 4)
    me_f = sec * 2 + quad
    sample = lax.div(lev, 2) * 2 + sec
    gs, gr, near, far, ag = (gs0, gs1), (gr0, gr1), (near0, near1), (far0, far1), (ag0, ag1)

    def of_group(q):
        return (lax.div(q, 2), tile, lax.rem(q, 2))

    def of_plane(q):
        return (lax.div(q, 8), z_lo * 8 + lax.rem(q, 8), sec)

    def of_near(q):
        return (lev, (quad * 4 + q) * 8 + spot, sec)

    def of_far(q):
        return (lev, (lax.rem(q, 2) * 4 + pos) * 8 + spot, lax.div(q, 2))

    above = (lev + 1 - 2 * r, lax.rem(tile + r, TILES), sec)
    below_dev = (lev + 1 - 2 * r, lax.rem(tile + TILES - 1 + r, TILES), sec)

    fetches = [
        pltpu.make_async_copy(src, dst, wsem.at[i])
        for i, (src, dst) in enumerate(
            (
                (surface.at[sample], sv), (cot_surface.at[sample], cv), (land_sea, mv), (bias, bv),
                (w_in_h, w_in), (w_mid_h, w_mid), (w_out_h, w_out_t),
            )
        )
    ]
    for copy in fetches:
        copy.start()

    barrier = pltpu.get_barrier_semaphore()

    def greet(where):
        pl.semaphore_signal(barrier, inc=1, device_id=where, device_id_type=MESH)

    def each(n, me, act):
        def go(p, c):
            act(lax.rem(me + p, n))
            return c

        lax.fori_loop(1, n, go, 0)

    each(GROUP, me_g, lambda q: greet(of_group(q)))
    greet(above)
    greet(below_dev)
    each(PLANE, me_p, lambda q: greet(of_plane(q)))
    each(4, pos, lambda q: greet(of_near(q)))
    each(4, me_f, lambda q: greet(of_far(q)))

    def pack(dst, g, uv, t, rest):
        dst[g, :, 0:384] = uv.astype(BF)
        dst[g, :, 384:512] = jnp.concatenate([t[:, 0:128], t[:, 256:384]], axis=0).astype(BF)
        dst[g, :, 512:640] = jnp.concatenate([t[:, 128:256], rest], axis=0).astype(BF)

    def unpack(slab):
        uv, one, two = slab[:, 0:384], slab[:, 384:512], slab[:, 512:640]
        t = jnp.concatenate([one[0:8], two[0:8], one[8:16]], axis=1)
        return uv[0:8], uv[8:16], t, two[8:16]

    nothing = jnp.zeros((8, 128), F32)
    for g in range(GROUP):
        for base, dst in ((0, a_s), (24, b_s)):
            wide = sent[g, base : base + 24, :].astype(F32)
            pack(dst, g, wide[0:16], wide[16:24], nothing)
    pl.semaphore_wait(barrier, GROUP - 1 + 2 + PLANE - 1 + 3 + 3)

    def push(src, dst, k, where):
        pushed.add(k)
        pltpu.make_async_remote_copy(
            src_ref=src, dst_ref=dst, send_sem=sems.at[2 * k], recv_sem=sems.at[2 * k + 1],
            device_id=where, device_id_type=MESH,
        ).start()

    def finish(ref, sem):
        pltpu.make_async_copy(ref, ref, sem).wait()

    pushed, taken, halos_sent, halos_taken = set(), set(), set(), set()

    def done(ref, i):
        taken.add(i)
        finish(ref, sems.at[i])

    def leave():
        sizes = (
            ra.at[pl.ds(0, 7)], rb.at[pl.ds(0, 7)], f_r.at[pl.ds(0, 7)], o_r.at[pl.ds(0, 7)],
            gr0.at[pl.ds(0, PLANE - 1)], gr1.at[pl.ds(0, PLANE - 1)], near0.at[pl.ds(0, 3)], near1.at[pl.ds(0, 3)],
            far0.at[pl.ds(0, 3)], far1.at[pl.ds(0, 3)],
            ag0.at[pl.ds(0, (PLANE - 1) * SHARE[0])], ag1.at[pl.ds(0, (PLANE - 1) * SHARE[1])],
        )
        for k in sorted(pushed):
            done(sizes[k], 2 * k)
            if 2 * k + 1 not in taken:
                done(sizes[k], 2 * k + 1)
        for k in sorted(halos_sent):
            for way in (0, 1):
                finish(hs.at[k], hsem.at[k, way, 0])
                if k not in halos_taken:
                    finish(hr.at[k, way], hsem.at[k, way, 1])

    each(GROUP, me_g, lambda q: push(a_s.at[q], ra.at[me_g], 0, of_group(q)))
    each(GROUP, me_g, lambda q: push(b_s.at[q], rb.at[me_g], 1, of_group(q)))

    lane = lax.broadcasted_iota(jnp.int32, (64, LANES), 1)
    real = lane < NLON
    level = lax.broadcasted_iota(jnp.int32, (64, LANES), 0).astype(F32)
    weight = 1.0 / (level + 1.0)
    row_i = lax.broadcasted_iota(jnp.int32, (64, 64), 0)
    col_i = lax.broadcasted_iota(jnp.int32, (64, 64), 1)
    tri_rise = jnp.where(row_i >= col_i, 1.0, 0.0).astype(F32)
    tri_fall = jnp.where(row_i <= col_i, 1.0, 0.0).astype(F32)
    x_factor, sin_lat = consts[0:1, :], consts[1:2, :]
    has_before, has_after = consts[2:3, :] > 0, consts[3:4, :] > 0

    def rising(values):
        return jnp.dot(tri_rise, values, precision=HIGH, preferred_element_type=F32)

    def falling(values):
        return jnp.dot(tri_fall, values, precision=HIGH, preferred_element_type=F32)

    def dx(values):
        rows = values.shape[0]
        ln = lax.broadcasted_iota(jnp.int32, (rows, LANES), 1)
        full = jnp.where(ln == NLON, pltpu.roll(values, NLON, 1), values)
        full = jnp.where(ln == LANES - 1, pltpu.roll(values, LANES - NLON, 1), full)
        return (pltpu.roll(full, LANES - 1, 1) - pltpu.roll(full, 1, 1)) * x_factor

    def halo_send(k, first, second):
        halos_sent.add(k)
        hs[k, 0:64, :] = first.astype(BF)
        hs[k, 64:128, :] = second.astype(BF)
        for way, where in ((0, above), (1, below_dev)):
            pltpu.make_async_remote_copy(
                src_ref=hs.at[k], dst_ref=hr.at[k, way], send_sem=hsem.at[k, way, 0],
                recv_sem=hsem.at[k, way, 1], device_id=where, device_id_type=MESH,
            ).start()

    def halo_take(k):
        halos_taken.add(k)
        for way in (0, 1):
            finish(hr.at[k, way], hsem.at[k, way, 1])
        before, after = hr[k, 0].astype(F32), hr[k, 1].astype(F32)
        zero = jnp.zeros((), F32)
        diff = (jnp.where(has_after, after, zero) - jnp.where(has_before, before, zero)) * 0.5
        return diff[0:64], diff[64:128]

    def forward(k):
        pre = dot(w_in_t[...], xs[k, 0:192, :]) + bmat[...]
        keep(pre, a1, s1, k)
        keep(dot(w_mid_t[...], a1[k]), a2, s2, k)
        return dot(w_out_t[...], a2[k]).astype(BF).astype(F32)

    def keep(pre, act, slope, k):
        cumulative = 0.5 * (1.0 + lax.erf(pre * INV_SQRT_TWO))
        density = jnp.exp(-0.5 * pre * pre) * INV_SQRT_TWO_PI
        act[k] = (pre * cumulative).astype(BF)
        slope[k] = cumulative + pre * density

    def backward(k, tend_bar):
        second_bar = (dot(w_out[...], tend_bar) * s2[k]).astype(BF)
        first_bar = (dot(w_mid[...], second_bar) * s1[k]).astype(BF)
        return second_bar, first_bar, dot(w_in[...], first_bar).astype(BF).astype(F32)

    def gradients(k, tend_bar, second_bar, first_bar):
        return (
            (0, dot_last(tend_bar, a2[k])),
            (192, dot_last(a1[k], second_bar)),
            (576, dot_last(xs[k], first_bar)),
        )

    def dynamics(surf, dv, dh):
        u, v, t = st[0:64, :], st[64:128, :], st[128:192, :]
        div = dx(u) + dv
        height = falling(weight * t) + surf
        flux = rising(div) * (1.0 / NLEV)
        return (
            -dx(height) + sin_lat * v, -dh - sin_lat * u, -flux,
            jnp.sum(div, axis=0, keepdims=True) * (-1.0 / NLEV),
        )

    def div_bar(surf_bar):
        return (-falling(br[128:192, :]) - surf_bar) * (1.0 / NLEV)

    def adjoint(surf_bar, da, ddb):
        a_u, a_v = br[0:64, :], br[64:128, :]
        hb = dx(a_u) + da
        return (
            -dx(div_bar(surf_bar)) - sin_lat * a_v, -ddb + sin_lat * a_u, weight * rising(hb),
            jnp.sum(hb, axis=0, keepdims=True),
        )

    def give(src, change, surf_change, dst, k):
        high = surf_change.astype(BF)
        low = (surf_change - high.astype(F32)).astype(BF)
        rows = lax.broadcasted_iota(jnp.int32, (8, 128), 0)
        tail = nothing
        for i in range(6):
            block = (high, low)[i // 3].astype(F32)[:, 128 * (i % 3) : 128 * (i % 3) + 128]
            tail = jnp.where(rows == i, block, tail)
        for g in range(GROUP):
            u, v, t = (change[f * 64 + g * 8 : f * 64 + g * 8 + 8, :] for f in range(3))
            pack(src, g, jnp.concatenate([u, v], axis=0), t, tail)
        dst[me_g] = src[me_g]
        each(GROUP, me_g, lambda q: push(src.at[q], dst.at[me_g], k, of_group(q)))

    ra[me_g] = a_s[me_g]
    rb[me_g] = b_s[me_g]
    for copy in fetches:
        copy.wait()
    flat[...] = jnp.zeros_like(flat)
    flat[0:1, 0:NLON] = jnp.where(r == 0, sv[0:1, :], sv[1:2, :])
    flat[1:2, 0:NLON] = TIME_STEP * jnp.where(r == 0, cv[0:1, :], cv[1:2, :])
    flat[2:3, 0:NLON] = jnp.where(jnp.where(r == 0, mv[0:1, :], mv[1:2, :]) > 0, 1.0, 0.0)
    land = flat[2:3, :] > 0
    mask_row = lax.broadcasted_iota(jnp.int32, (16, LANES), 0)
    sea_or_land = jnp.where(land, 1, 0)
    hot = jnp.where((mask_row == sea_or_land) & (lax.broadcasted_iota(jnp.int32, (16, LANES), 1) < NLON), 1.0, 0.0)
    xs[0, 192:208, :] = hot.astype(BF)
    xs[1, 192:208, :] = hot.astype(BF)
    bias_row = lax.broadcasted_iota(jnp.int32, (8, 384), 0)
    both = jnp.where(bias_row == 0, bv[0:1, :], jnp.where(bias_row == 1, bv[1:2, :], 0.0))
    bmat[...] = lax.dot_general(both, hot[0:8], (((0,), (0,)), ((), ())), precision=HIGH, preferred_element_type=F32)
    w_in_t[...] = w_in[...].T
    w_mid_t[...] = w_mid[...].T
    w_out[...] = w_out_t[...].T
    surf0, sbar0 = flat[0:1, :], flat[1:2, :]

    done(ra.at[pl.ds(0, 7)], 1)
    for g in range(GROUP):
        u, v, t, _ = unpack(ra[g].astype(F32))
        for f, part in enumerate((u, v, t)):
            st[f * 64 + g * 8 : f * 64 + g * 8 + 8, :] = part
    halo_send(0, st[64:128, :], falling(weight * st[128:192, :]) + surf0)
    xs[0, 0:192, :] = st[...].astype(BF)
    tend = forward(0)

    done(rb.at[pl.ds(0, 7)], 3)
    for g in range(GROUP):
        u, v, t, _ = unpack(rb[g].astype(F32))
        for f, part in enumerate((u, v, t)):
            br[f * 64 + g * 8 : f * 64 + g * 8 + 8, :] = part
    halo_send(1, br[64:128, :], div_bar(sbar0))

    du, dv, dt, dsurf = dynamics(surf0, *halo_take(0))
    for i, d in enumerate((du, dv, dt)):
        at = slice(64 * i, 64 * i + 64)
        change = TIME_STEP * (d + tend[at])
        inc[at, :] = change
        st[at, :] = st[at, :] + change
    surf_inc = TIME_STEP * dsurf
    surf1 = surf0 + surf_inc
    halo_send(2, st[64:128, :], falling(weight * st[128:192, :]) + surf1)
    xs[1, 0:192, :] = st[...].astype(BF)
    tend = forward(1)

    t0 = br[...].astype(BF)
    second_bar, first_bar, input_bar = backward(1, t0)
    au, av, at_, asurf = adjoint(sbar0, *halo_take(1))
    for i, d in enumerate((au, av, at_)):
        at = slice(64 * i, 64 * i + 64)
        change = d + input_bar[at]
        ginc[at, :] = change
        br[at, :] = jnp.where(real, br[at, :] + TIME_STEP * change, 0.0)
    gsurf = asurf
    sbar1 = sbar0 + TIME_STEP * asurf
    halo_send(3, br[64:128, :], div_bar(sbar1))

    du, dv, dt, dsurf = dynamics(surf1, *halo_take(2))
    for i, d in enumerate((du, dv, dt)):
        at = slice(64 * i, 64 * i + 64)
        inc[at, :] = inc[at, :] + TIME_STEP * (d + tend[at])
    give(f_s, inc, surf_inc + TIME_STEP * dsurf, f_r, 2)

    for at, g in gradients(1, t0, second_bar, first_bar):
        gacc[at : at + g.shape[0], :] = g

    def share(ref, q, part):
        return ref.at[pl.ds(pl.multiple_of(q * SHARE[part], 16), SHARE[part])]

    def stage(total, at, part):
        for b in range(3):
            base = PART[part] * b + at
            gs[part][base : base + total.shape[0], :] = total[:, 128 * b : 128 * b + 128].astype(BF)

    def scatter(part):
        each(PLANE, me_p, lambda q: push(share(gs[part], q, part), gr[part].at[me_p], 4 + part, of_plane(q)))

    gs1[3 * PART[1] :, :] = jnp.zeros((PLANE * SHARE[1] - 3 * PART[1], 128), BF)
    t1 = br[...].astype(BF)
    second_bar = (dot(w_out[...], t1) * s2[0]).astype(BF)
    stage(gacc[0:192, :] + dot_last(t1, a2[0]), 0, 0)
    mid = gacc[192:576, :] + dot_last(a1[0], second_bar)
    stage(mid[0:320], 192, 0)
    stage(mid[320:384], 0, 1)
    scatter(0)
    first_bar = (dot(w_mid[...], second_bar) * s1[0]).astype(BF)
    stage(gacc[576:784, :] + dot_last(xs[0], first_bar), 64, 1)
    scatter(1)
    input_bar = dot(w_in[...], first_bar).astype(BF).astype(F32)

    au, av, at_, asurf = adjoint(sbar1, *halo_take(3))
    for i, d in enumerate((au, av, at_)):
        at = slice(64 * i, 64 * i + 64)
        ginc[at, :] = ginc[at, :] + d + input_bar[at]
    give(o_s, ginc, gsurf + asurf, o_r, 3)

    def sum_plane(part):
        done(gr[part].at[pl.ds(0, PLANE - 1)], 2 * (4 + part) + 1)
        mine = gs[part][pl.ds(pl.multiple_of(me_p * SHARE[part], 16), SHARE[part]), :].astype(F32)
        near[part][pos] = lax.fori_loop(
            1, PLANE, lambda p, acc: acc + gr[part][lax.rem(me_p + p, PLANE)].astype(F32), mine
        )
        each(4, pos, lambda q: push(near[part].at[pos], near[part].at[pos], 6 + part, of_near(q)))

    def sum_near(part):
        done(near[part].at[pl.ds(0, 3)], 2 * (6 + part) + 1)
        n = near[part]
        far[part][me_f] = ((n[0] + n[1]) + (n[2] + n[3])).astype(BF)
        each(4, me_f, lambda q: push(far[part].at[me_f], far[part].at[me_f], 8 + part, of_far(q)))

    def sum_far(part):
        done(far[part].at[pl.ds(0, 3)], 2 * (8 + part) + 1)
        f = [far[part][i].astype(F32) for i in range(4)]
        at = pl.ds(pl.multiple_of(me_p * SHARE[part], 16), SHARE[part])
        ag[part][at, :] = ((f[0] + f[1]) + (f[2] + f[3])).astype(BF)
        each(PLANE, me_p, lambda q: push(share(ag[part], me_p, part), share(ag[part], me_p, part), 10 + part, of_plane(q)))

    sum_plane(0)
    sum_plane(1)
    sum_near(0)
    sum_near(1)
    sum_far(0)
    sum_far(1)

    def columns_out(came, out):
        for g in range(GROUP):
            u, v, t, rest = unpack(came[g].astype(F32))
            high = jnp.concatenate([rest[0:1], rest[1:2], rest[2:3]], axis=1)
            low = jnp.concatenate([rest[3:4], rest[4:5], rest[5:6]], axis=1)
            row = lax.broadcasted_iota(jnp.int32, (8, LANES), 0)
            tail = jnp.where(row == 0, high, jnp.where(row == 1, low, 0.0))
            out[g] = jnp.concatenate([u, v, t, tail], axis=0).astype(BF)

    done(f_r.at[pl.ds(0, 7)], 5)
    columns_out(f_r, out_f)
    done(o_r.at[pl.ds(0, 7)], 7)
    columns_out(o_r, out_g)

    def taken_from(part, b, first, last):
        base = PART[part] * b
        return ag[part][base + first : base + last, :].astype(F32)

    done(ag0.at[pl.ds(0, (PLANE - 1) * SHARE[0])], 21)
    for b in range(3):
        lanes = slice(128 * b, 128 * b + 128)
        g_out[:, lanes] = taken_from(0, b, 0, 192)
        g_mid[0:320, lanes] = taken_from(0, b, 192, 512)
    done(ag1.at[pl.ds(0, (PLANE - 1) * SHARE[1])], 23)
    for b in range(3):
        lanes = slice(128 * b, 128 * b + 128)
        g_mid[320:384, lanes] = taken_from(1, b, 0, 64)
        g_in[:, lanes] = taken_from(1, b, 64, 256)
        g_bias[:, lanes] = taken_from(1, b, 256, 272)[0:2]
    leave()


def call(*operands):
    def v(shape, dtype):
        return pltpu.VMEM(shape, dtype)

    slab = (GROUP, *SLAB)
    hidden = (2, 384, LANES)
    hbm, vmem = pl.BlockSpec(memory_space=pl.ANY), pl.BlockSpec(memory_space=pltpu.VMEM)
    return pl.pallas_call(
        kernel,
        out_shape=(
            jax.ShapeDtypeStruct((GROUP, 32, LANES), BF),
            jax.ShapeDtypeStruct((GROUP, 32, LANES), BF),
            jax.ShapeDtypeStruct((192, 384), F32),
            jax.ShapeDtypeStruct((384, 384), F32),
            jax.ShapeDtypeStruct((192, 384), F32),
            jax.ShapeDtypeStruct((2, 384), F32),
        ),
        in_specs=[vmem] * 2 + [hbm] * 7,
        out_specs=tuple([vmem] * 6),
        scratch_shapes=[
            v((192, 384), BF), v((384, 384), BF), v((384, 192), BF),
            v((384, 192), BF), v((384, 384), BF), v((192, 384), BF),
            v((2, NLON), F32), v((2, NLON), F32), v((2, NLON), jnp.int32), v((2, 384), F32),
            v((8, LANES), F32), v((384, LANES), F32),
            v(slab, BF), v(slab, BF), v(slab, BF), v(slab, BF),
            v((4, 128, LANES), BF), v((4, 2, 128, LANES), BF),
            v((192, LANES), F32), v((192, LANES), F32), v((2, 208, LANES), BF),
            v(hidden, BF), v(hidden, BF), v(hidden, F32), v(hidden, F32),
            v((192, LANES), F32), v((192, LANES), F32),
            v(slab, BF), v(slab, BF), v(slab, BF), v(slab, BF),
            v((GROWS, 384), F32),
            v((PLANE * SHARE[0], 128), BF), v((PLANE * SHARE[1], 128), BF),
            v((PLANE, SHARE[0], 128), BF), v((PLANE, SHARE[1], 128), BF),
            v((4, SHARE[0], 128), F32), v((4, SHARE[1], 128), F32),
            v((4, SHARE[0], 128), BF), v((4, SHARE[1], 128), BF),
            v((PLANE * SHARE[0], 128), BF), v((PLANE * SHARE[1], 128), BF),
            pltpu.SemaphoreType.DMA((24,)), pltpu.SemaphoreType.DMA((4, 2, 2)), pltpu.SemaphoreType.DMA((7,)),
        ],
        compiler_params=pltpu.CompilerParams(
            collective_id=0, has_side_effects=True, vmem_limit_bytes=40 * 2**20
        ),
        name="window",
    )(*operands)


def on_device(fields, surface, cot_fields, cot_surface, land_sea, w_in, w_mid, w_out, bias_in):
    lev_i, tile_i = lax.axis_index("lev"), lax.axis_index("tile")
    row_in_band = lax.rem(lev_i, 2)
    row = tile_i * 2 + row_in_band
    latitude = -0.5 * math.pi + (row.astype(F32) + 0.5) * (math.pi / (2 * TILES))
    x_factor = 0.5 / jnp.maximum(jnp.cos(latitude), COS_FLOOR)
    sin_lat = jnp.sin(latitude)

    def pad(values):
        return jnp.pad(values, [(0, 0)] * (values.ndim - 1) + [(0, LANES - NLON)])

    def to_columns(values):
        split = values.astype(BF).reshape(3, 8, 2, 2, 2, NLON)
        return pad(split.transpose(2, 4, 3, 0, 1, 5).reshape(8, 24, NLON))

    sent = jnp.concatenate([to_columns(fields), to_columns(TIME_STEP * cot_fields)], axis=1)
    consts = jnp.stack([x_factor, sin_lat, (row > 0).astype(F32), (row < 2 * TILES - 1).astype(F32)])
    consts = jnp.broadcast_to(jnp.concatenate([consts, consts])[:, None], (8, LANES))
    came_f, came_g, g_in, g_mid, g_out, g_bias = call(
        sent, consts, surface, cot_surface, land_sea, bias_in, w_in, w_mid, w_out.T
    )

    def returned(came):
        came = came[:, :, :NLON].astype(F32)
        levels = came[:, :24].reshape(2, 2, 2, 3, 8, NLON).transpose(3, 4, 0, 2, 1, 5).reshape(3, 8, 4, 2, NLON)
        level_flat = (came[:, 24] + came[:, 25]).reshape(2, 2, 2, NLON).transpose(0, 2, 1, 3).reshape(4, 2, NLON)
        return levels, level_flat

    df, ds = returned(came_f)
    dg, dgs = returned(came_g)
    return (
        fields + df,
        surface + ds,
        cot_fields + dg,
        cot_surface + dgs,
        g_in,
        g_mid,
        g_out.T,
        g_bias,
    )


def solution(mesh):
    levels = P(None, ("lev", "sec"), None, "tile", None)
    flat = P(None, "tile", None)
    return jax.shard_map(
        on_device,
        mesh=mesh,
        in_specs=(levels, flat, levels, flat, P("tile", None), P(), P(), P(), P()),
        out_specs=(levels, flat, levels, flat, P(), P(), P(), P()),
        check_vma=False,
    )
```

time: 105 us -> 102 us (0.971)
  local copies, waits for them, and re-layouts: 7.96 us -> 5.23 us
    unnamed x22, local copies, waits for them, and re-layouts: 6.01 us -> 4.64 us
    slice x3 -> x0, local copies, waits for them, and re-layouts: 1.33 us -> none  [the longest x1 0.73 us: on_device(): g_in[:192]]
where the time goes in v3:
time: 102 us; the launch traced here: 101 us
  Pallas kernels  90.7 us (89%)
  local copies, waits for them, and re-layouts  5.23 us (5%)
  other arithmetic  4.42 us (4%)
  between operations  1.03 us (1%)
    pallas_call x1, Pallas kernels, call(): pl.pallas_call(kernel, out_shape=(jax.ShapeDtypeStruct((GROUP, 32, LANES)...  90.7 us
    unnamed x22, local copies, waits for them, and re-layouts  4.64 us

profile of v3, /device:TPU:1, one launch (start us, length us, event | category | flops | bytes accessed | tf_op | source)
XLA Modules:
  0.0 101.3 jit_solution(18246639693383283018)
XLA Ops:
  0.8 0.1 concatenate.8
  0.9 0.1 broadcast_in_dim.2.consts
  1.0 0.0 copy-start.7
  1.0 1.1 %convert_element_type.20 = bf16[3,8,4,2,360]{4,3,2,1,0:T(2,128)(2,1)S(1)} convert(f32[3,8,4,2,360]{4,3,2,1,0:T(2,128)} %param.9) | non-fusion elementwise | flops 69120 | bytes 414720 | tf_op jit(solution)/shard_map/convert_element_type | solution.py:475
  2.1 0.0 copy-done.7
  2.2 0.2 multiply_convert_fusion
  2.3 0.0 copy-start.3
  2.3 0.0 copy-start.4
  2.3 0.0 copy-start.5
  2.4 0.0 copy-start.6
  2.4 0.0 copy-start
  2.4 0.0 copy-start.1
  2.4 0.0 copy-start.2
  2.5 0.6 copy-done.3
  3.0 0.0 copy-done.4
  3.0 0.0 copy-done.5
  3.0 0.0 copy-done.6
  3.1 0.3 copy-done
  3.4 0.0 copy-done.1
  3.4 0.1 copy-done.2
  3.5 90.7 %window.1 = (bf16[8,32,384]{2,1,0:T(8,128)(2,1)S(1)}, bf16[8,32,384]{2,1,0:T(8,128)(2,1)S(1)}, f32[192,384]{1,0:T(8,128)S(1)}, f32[384,384]{1,0:T(8,128)S(1)}, f...) custom-call(bf16[8,48,384]{2,1,0:T(8,128)(2,1)S(1)} %fusion.2.sent, f32[8,384]{1,0:T(8,128)S(1)} %broadcast_in_dim.2.consts, ...), custom_call_target="tpu_custom_call" | custom-call | tf_op jit(solution)/shard_map/window/pallas_call | solution.py:425
  94.1 0.1 slice_convert_fusion
  94.3 0.2 copy.21
  94.5 0.9 add.42
  95.3 0.6 bitcast_add_fusion
  96.0 0.0 copy-start.8
  96.0 0.2 copy.19
  96.2 0.8 copy-done.8
  97.0 0.9 add.38
  97.9 0.6 bitcast_add_fusion.1
  98.5 0.7 copy.29
  99.2 0.8 copy.30
  100.0 0.7 copy.31
  100.8 0.6 copy.32
  (11 shorter events, 0.2 us)
Async XLA Ops:
  1.0 1.1 %copy-start.7 = (f32[3,8,4,2,360]{4,3,2,1,0:T(2,128)S(1)}, f32[3,8,4,2,360]{4,3,2,1,0:T(2,128)}, u32[]{:S(2)}) copy-start(f32[3,8,4,2,360]{4,3,2,1,0:T(2,128)} %param.11) | copy-start | bytes 829444
  2.3 0.7 copy-start.3
  2.3 0.7 copy-start.4
  2.3 0.7 copy-start.5
  2.4 0.7 copy-start.6
  2.4 1.0 copy-start
  2.4 1.0 copy-start.1
  2.4 1.1 %copy-start.2 = (bf16[384,192]{0,1:T(8,128)(2,1)S(1)}, bf16[384,192]{0,1:T(8,128)(2,1)}, u32[]{:S(2)}) copy-start(bf16[384,192]{0,1:T(8,128)(2,1)} %param.16) | copy-start | bytes 442372
  96.0 1.0 copy-start.8

commit v4 on v3

--- a/solution.py
+++ b/solution.py
@@ -37,7 +37,7 @@
     sent, consts, surface, cot_surface, land_sea, bias, w_in_h, w_mid_h, w_out_h,
     out_f, out_g, g_in, g_mid, g_out, g_bias,
     w_in, w_mid, w_out, w_in_t, w_mid_t, w_out_t, sv, cv, mv, bv, flat, bmat,
-    a_s, b_s, ra, rb, hs, hr, st, br, xs, a1, a2, s1, s2, inc, ginc,
+    pre, hgt, dbr, a_s, b_s, ra, rb, hs, hr, st, br, xs, a1, a2, s1, s2, inc, ginc,
     f_s, f_r, o_s, o_r, gacc, gs0, gs1, gr0, gr1, near0, near1, far0, far1, ag0, ag1,
     sems, hsem, wsem,
 ):
@@ -46,7 +46,10 @@
     me_g = lev * 2 + sec
     spot = lax.rem(tile, 8)
     z_lo = lax.div(tile, 8)
-    me_p = lev * 8 + spot
+    core = lax.rem(spot, 2)
+    me_c = lev * 4 + lax.div(spot, 2)
+    me_p = core * 16 + me_c
+    mate = (lev, tile + 1 - 2 * core, sec)
     pos = lax.rem(z_lo, 4)
     quad = lax.div(z_lo, 4)
     me_f = sec * 2 + quad
@@ -57,7 +60,8 @@
         return (lax.div(q, 2), tile, lax.rem(q, 2))
 
     def of_plane(q):
-        return (lax.div(q, 8), z_lo * 8 + lax.rem(q, 8), sec)
+        chip = lax.rem(q, 16)
+        return (lax.div(chip, 4), z_lo * 8 + lax.rem(chip, 4) * 2 + lax.div(q, 16), sec)
 
     def of_near(q):
         return (lev, (quad * 4 + q) * 8 + spot, sec)
@@ -137,7 +141,8 @@
             ra.at[pl.ds(0, 7)], rb.at[pl.ds(0, 7)], f_r.at[pl.ds(0, 7)], o_r.at[pl.ds(0, 7)],
             gr0.at[pl.ds(0, PLANE - 1)], gr1.at[pl.ds(0, PLANE - 1)], near0.at[pl.ds(0, 3)], near1.at[pl.ds(0, 3)],
             far0.at[pl.ds(0, 3)], far1.at[pl.ds(0, 3)],
-            ag0.at[pl.ds(0, (PLANE - 1) * SHARE[0])], ag1.at[pl.ds(0, (PLANE - 1) * SHARE[1])],
+            ag0.at[pl.ds(0, 15 * SHARE[0])], ag1.at[pl.ds(0, 15 * SHARE[1])],
+            ag0.at[pl.ds(0, 16 * SHARE[0])], ag1.at[pl.ds(0, 16 * SHARE[1])],
         )
         for k in sorted(pushed):
             done(sizes[k], 2 * k)
@@ -156,18 +161,26 @@
     real = lane < NLON
     level = lax.broadcasted_iota(jnp.int32, (64, LANES), 0).astype(F32)
     weight = 1.0 / (level + 1.0)
-    row_i = lax.broadcasted_iota(jnp.int32, (64, 64), 0)
-    col_i = lax.broadcasted_iota(jnp.int32, (64, 64), 1)
-    tri_rise = jnp.where(row_i >= col_i, 1.0, 0.0).astype(F32)
-    tri_fall = jnp.where(row_i <= col_i, 1.0, 0.0).astype(F32)
+    row_i = lax.broadcasted_iota(jnp.int32, (64, 192), 0)
+    col_i = lax.broadcasted_iota(jnp.int32, (64, 192), 1)
+    col_i = jnp.where(col_i >= 128, col_i - 128, jnp.where(col_i >= 64, col_i - 64, col_i))
+    tri_rise = jnp.where(row_i >= col_i, 1.0, 0.0).astype(BF)
+    tri_fall = jnp.where(row_i <= col_i, 1.0, 0.0).astype(BF)
     x_factor, sin_lat = consts[0:1, :], consts[1:2, :]
     has_before, has_after = consts[2:3, :] > 0, consts[3:4, :] > 0
 
+    def vertical(which, values):
+        one = values.astype(BF)
+        rest = values - one.astype(F32)
+        two = rest.astype(BF)
+        three = (rest - two.astype(F32)).astype(BF)
+        return dot(which, jnp.concatenate([one, two, three], axis=0))
+
     def rising(values):
-        return jnp.dot(tri_rise, values, precision=HIGH, preferred_element_type=F32)
+        return vertical(tri_rise, values)
 
     def falling(values):
-        return jnp.dot(tri_fall, values, precision=HIGH, preferred_element_type=F32)
+        return vertical(tri_fall, values)
 
     def dx(values):
         rows = values.shape[0]
@@ -196,16 +209,23 @@
         return diff[0:64], diff[64:128]
 
     def forward(k):
-        pre = dot(w_in_t[...], xs[k, 0:192, :]) + bmat[...]
-        keep(pre, a1, s1, k)
-        keep(dot(w_mid_t[...], a1[k]), a2, s2, k)
+        pre[...] = dot(w_in_t[...], xs[k, 0:192, :])
+        keep(a1, s1, k, True)
+        pre[...] = dot(w_mid_t[...], a1[k])
+        keep(a2, s2, k, False)
         return dot(w_out_t[...], a2[k]).astype(BF).astype(F32)
 
-    def keep(pre, act, slope, k):
-        cumulative = 0.5 * (1.0 + lax.erf(pre * INV_SQRT_TWO))
-        density = jnp.exp(-0.5 * pre * pre) * INV_SQRT_TWO_PI
-        act[k] = (pre * cumulative).astype(BF)
-        slope[k] = cumulative + pre * density
+    def keep(act, slope, k, biased):
+        def block(i, c):
+            rows = pl.ds(pl.multiple_of(i * 32, 32), 32)
+            value = pre[rows, :] + bmat[rows, :] if biased else pre[rows, :]
+            cumulative = 0.5 * (1.0 + lax.erf(value * INV_SQRT_TWO))
+            density = jnp.exp(-0.5 * value * value) * INV_SQRT_TWO_PI
+            act[k, rows, :] = (value * cumulative).astype(BF)
+            slope[k, rows, :] = cumulative + value * density
+            return c
+
+        lax.fori_loop(0, 12, block, 0)
 
     def backward(k, tend_bar):
         second_bar = (dot(w_out[...], tend_bar) * s2[k]).astype(BF)
@@ -219,24 +239,23 @@
             (576, dot_last(xs[k], first_bar)),
         )
 
-    def dynamics(surf, dv, dh):
-        u, v, t = st[0:64, :], st[64:128, :], st[128:192, :]
+    def dynamics(dv, dh):
+        u, v = st[0:64, :], st[64:128, :]
         div = dx(u) + dv
-        height = falling(weight * t) + surf
         flux = rising(div) * (1.0 / NLEV)
         return (
-            -dx(height) + sin_lat * v, -dh - sin_lat * u, -flux,
+            -dx(hgt[...]) + sin_lat * v, -dh - sin_lat * u, -flux,
             jnp.sum(div, axis=0, keepdims=True) * (-1.0 / NLEV),
         )
 
     def div_bar(surf_bar):
         return (-falling(br[128:192, :]) - surf_bar) * (1.0 / NLEV)
 
-    def adjoint(surf_bar, da, ddb):
+    def adjoint(da, ddb):
         a_u, a_v = br[0:64, :], br[64:128, :]
         hb = dx(a_u) + da
         return (
-            -dx(div_bar(surf_bar)) - sin_lat * a_v, -ddb + sin_lat * a_u, weight * rising(hb),
+            -dx(dbr[...]) - sin_lat * a_v, -ddb + sin_lat * a_u, weight * rising(hb),
             jnp.sum(hb, axis=0, keepdims=True),
         )
 
@@ -281,7 +300,8 @@
         u, v, t, _ = unpack(ra[g].astype(F32))
         for f, part in enumerate((u, v, t)):
             st[f * 64 + g * 8 : f * 64 + g * 8 + 8, :] = part
-    halo_send(0, st[64:128, :], falling(weight * st[128:192, :]) + surf0)
+    hgt[...] = falling(weight * st[128:192, :]) + surf0
+    halo_send(0, st[64:128, :], hgt[...])
     xs[0, 0:192, :] = st[...].astype(BF)
     tend = forward(0)
 
@@ -290,9 +310,10 @@
         u, v, t, _ = unpack(rb[g].astype(F32))
         for f, part in enumerate((u, v, t)):
             br[f * 64 + g * 8 : f * 64 + g * 8 + 8, :] = part
-    halo_send(1, br[64:128, :], div_bar(sbar0))
-
-    du, dv, dt, dsurf = dynamics(surf0, *halo_take(0))
+    dbr[...] = div_bar(sbar0)
+    halo_send(1, br[64:128, :], dbr[...])
+
+    du, dv, dt, dsurf = dynamics(*halo_take(0))
     for i, d in enumerate((du, dv, dt)):
         at = slice(64 * i, 64 * i + 64)
         change = TIME_STEP * (d + tend[at])
@@ -300,13 +321,14 @@
         st[at, :] = st[at, :] + change
     surf_inc = TIME_STEP * dsurf
     surf1 = surf0 + surf_inc
-    halo_send(2, st[64:128, :], falling(weight * st[128:192, :]) + surf1)
+    hgt[...] = falling(weight * st[128:192, :]) + surf1
+    halo_send(2, st[64:128, :], hgt[...])
     xs[1, 0:192, :] = st[...].astype(BF)
     tend = forward(1)
 
     t0 = br[...].astype(BF)
     second_bar, first_bar, input_bar = backward(1, t0)
-    au, av, at_, asurf = adjoint(sbar0, *halo_take(1))
+    au, av, at_, asurf = adjoint(*halo_take(1))
     for i, d in enumerate((au, av, at_)):
         at = slice(64 * i, 64 * i + 64)
         change = d + input_bar[at]
@@ -314,9 +336,10 @@
         br[at, :] = jnp.where(real, br[at, :] + TIME_STEP * change, 0.0)
     gsurf = asurf
     sbar1 = sbar0 + TIME_STEP * asurf
-    halo_send(3, br[64:128, :], div_bar(sbar1))
-
-    du, dv, dt, dsurf = dynamics(surf1, *halo_take(2))
+    dbr[...] = div_bar(sbar1)
+    halo_send(3, br[64:128, :], dbr[...])
+
+    du, dv, dt, dsurf = dynamics(*halo_take(2))
     for i, d in enumerate((du, dv, dt)):
         at = slice(64 * i, 64 * i + 64)
         inc[at, :] = inc[at, :] + TIME_STEP * (d + tend[at])
@@ -349,7 +372,7 @@
     scatter(1)
     input_bar = dot(w_in[...], first_bar).astype(BF).astype(F32)
 
-    au, av, at_, asurf = adjoint(sbar1, *halo_take(3))
+    au, av, at_, asurf = adjoint(*halo_take(3))
     for i, d in enumerate((au, av, at_)):
         at = slice(64 * i, 64 * i + 64)
         ginc[at, :] = ginc[at, :] + d + input_bar[at]
@@ -374,7 +397,14 @@
         f = [far[part][i].astype(F32) for i in range(4)]
         at = pl.ds(pl.multiple_of(me_p * SHARE[part], 16), SHARE[part])
         ag[part][at, :] = ((f[0] + f[1]) + (f[2] + f[3])).astype(BF)
-        each(PLANE, me_p, lambda q: push(share(ag[part], me_p, part), share(ag[part], me_p, part), 10 + part, of_plane(q)))
+        own = share(ag[part], me_p, part)
+        each(16, me_c, lambda q: push(own, own, 10 + part, of_plane(core * 16 + q)))
+
+    def to_mate(part):
+        done(ag[part].at[pl.ds(0, 15 * SHARE[part])], 2 * (10 + part) + 1)
+        rows = 16 * SHARE[part]
+        half = ag[part].at[pl.ds(pl.multiple_of(core * rows, 16), rows)]
+        push(half, half, 12 + part, mate)
 
     sum_plane(0)
     sum_plane(1)
@@ -392,8 +422,10 @@
             tail = jnp.where(row == 0, high, jnp.where(row == 1, low, 0.0))
             out[g] = jnp.concatenate([u, v, t, tail], axis=0).astype(BF)
 
+    to_mate(0)
     done(f_r.at[pl.ds(0, 7)], 5)
     columns_out(f_r, out_f)
+    to_mate(1)
     done(o_r.at[pl.ds(0, 7)], 7)
     columns_out(o_r, out_g)
 
@@ -401,12 +433,12 @@
         base = PART[part] * b
         return ag[part][base + first : base + last, :].astype(F32)
 
-    done(ag0.at[pl.ds(0, (PLANE - 1) * SHARE[0])], 21)
+    done(ag0.at[pl.ds(0, 16 * SHARE[0])], 25)
     for b in range(3):
         lanes = slice(128 * b, 128 * b + 128)
         g_out[:, lanes] = taken_from(0, b, 0, 192)
         g_mid[0:320, lanes] = taken_from(0, b, 192, 512)
-    done(ag1.at[pl.ds(0, (PLANE - 1) * SHARE[1])], 23)
+    done(ag1.at[pl.ds(0, 16 * SHARE[1])], 27)
     for b in range(3):
         lanes = slice(128 * b, 128 * b + 128)
         g_mid[320:384, lanes] = taken_from(1, b, 0, 64)
@@ -439,6 +471,7 @@
             v((384, 192), BF), v((384, 384), BF), v((192, 384), BF),
             v((2, NLON), F32), v((2, NLON), F32), v((2, NLON), jnp.int32), v((2, 384), F32),
             v((8, LANES), F32), v((384, LANES), F32),
+            v((384, LANES), F32), v((64, LANES), F32), v((64, LANES), F32),
             v(slab, BF), v(slab, BF), v(slab, BF), v(slab, BF),
             v((4, 128, LANES), BF), v((4, 2, 128, LANES), BF),
             v((192, LANES), F32), v((192, LANES), F32), v((2, 208, LANES), BF),
@@ -451,7 +484,7 @@
             v((4, SHARE[0], 128), F32), v((4, SHARE[1], 128), F32),
             v((4, SHARE[0], 128), BF), v((4, SHARE[1], 128), BF),
             v((PLANE * SHARE[0], 128), BF), v((PLANE * SHARE[1], 128), BF),
-            pltpu.SemaphoreType.DMA((24,)), pltpu.SemaphoreType.DMA((4, 2, 2)), pltpu.SemaphoreType.DMA((7,)),
+            pltpu.SemaphoreType.DMA((28,)), pltpu.SemaphoreType.DMA((4, 2, 2)), pltpu.SemaphoreType.DMA((7,)),
         ],
         compiler_params=pltpu.CompilerParams(
             collective_id=0, has_side_effects=True, vmem_limit_bytes=40 * 2**20

time: 102 us -> 101 us (level)
  no operation moved by 1% of the time
where the time goes in v4:
time: 101 us
  Pallas kernels  90.6 us (90%)
  local copies, waits for them, and re-layouts  5.23 us (5%)
  other arithmetic  4.42 us (4%)
  between operations  1.03 us (1%)
    pallas_call x1, Pallas kernels, call(): pl.pallas_call(kernel, out_shape=(jax.ShapeDtypeStruct((GROUP, 32, LANES)...  90.6 us
    unnamed x22, local copies, waits for them, and re-layouts  4.64 us

profile of v4, /device:TPU:1, one launch (start us, length us, event | category | flops | bytes accessed | tf_op | source)
XLA Modules:
  0.0 101.3 jit_solution(17841653261090860274)
XLA Ops:
  0.8 0.1 concatenate.8
  0.9 0.1 broadcast_in_dim.2.consts
  1.0 0.0 copy-start.7
  1.0 1.1 %convert_element_type.20 = bf16[3,8,4,2,360]{4,3,2,1,0:T(2,128)(2,1)S(1)} convert(f32[3,8,4,2,360]{4,3,2,1,0:T(2,128)} %param.9) | non-fusion elementwise | flops 69120 | bytes 414720 | tf_op jit(solution)/shard_map/convert_element_type | solution.py:508
  2.1 0.0 copy-done.7
  2.2 0.2 multiply_convert_fusion
  2.3 0.0 copy-start.3
  2.3 0.0 copy-start.4
  2.3 0.0 copy-start.5
  2.4 0.0 copy-start.6
  2.4 0.0 copy-start
  2.4 0.0 copy-start.1
  2.4 0.0 copy-start.2
  2.5 0.6 copy-done.3
  3.0 0.0 copy-done.4
  3.0 0.0 copy-done.5
  3.0 0.0 copy-done.6
  3.1 0.3 copy-done
  3.4 0.0 copy-done.1
  3.4 0.1 copy-done.2
  3.5 90.6 %window.1 = (bf16[8,32,384]{2,1,0:T(8,128)(2,1)S(1)}, bf16[8,32,384]{2,1,0:T(8,128)(2,1)S(1)}, f32[192,384]{1,0:T(8,128)S(1)}, f32[384,384]{1,0:T(8,128)S(1)}, f...) custom-call(bf16[8,48,384]{2,1,0:T(8,128)(2,1)S(1)} %fusion.2.sent, f32[8,384]{1,0:T(8,128)S(1)} %broadcast_in_dim.2.consts, ...), custom_call_target="tpu_custom_call" | custom-call | tf_op jit(solution)/shard_map/window/pallas_call | solution.py:457
  94.1 0.1 slice_convert_fusion
  94.3 0.2 copy.21
  94.4 0.9 add.42
  95.3 0.6 bitcast_add_fusion
  96.0 0.0 copy-start.8
  96.0 0.2 copy.19
  96.2 0.8 copy-done.8
  97.0 0.9 add.38
  97.9 0.6 bitcast_add_fusion.1
  98.5 0.7 copy.29
  99.2 0.8 copy.30
  100.0 0.7 copy.31
  100.7 0.6 copy.32
  (11 shorter events, 0.2 us)
Async XLA Ops:
  1.0 1.1 %copy-start.7 = (f32[3,8,4,2,360]{4,3,2,1,0:T(2,128)S(1)}, f32[3,8,4,2,360]{4,3,2,1,0:T(2,128)}, u32[]{:S(2)}) copy-start(f32[3,8,4,2,360]{4,3,2,1,0:T(2,128)} %param.11) | copy-start | bytes 829444
  2.3 0.7 copy-start.3
  2.3 0.7 copy-start.4
  2.3 0.7 copy-start.5
  2.4 0.7 copy-start.6
  2.4 1.0 copy-start
  2.4 1.0 copy-start.1
  2.4 1.1 %copy-start.2 = (bf16[384,192]{0,1:T(8,128)(2,1)S(1)}, bf16[384,192]{0,1:T(8,128)(2,1)}, u32[]{:S(2)}) copy-start(bf16[384,192]{0,1:T(8,128)(2,1)} %param.16) | copy-start | bytes 442372
  96.0 1.0 copy-start.8

commit v5 on v4

--- a/solution.py
+++ b/solution.py
@@ -33,16 +33,25 @@
     return lax.dot_general(a, b, (((1,), (1,)), ((), ())), preferred_element_type=F32)
 
 
+def row_of(lev, tile):
+    return lax.rem(lev + lax.rem(tile, 2), 2)
+
+
+def sample_half(lev, tile):
+    flip = lax.rem(tile, 2) * (1 - lax.rem(lev, 2))
+    return lax.rem(lax.div(lev, 2) + lax.rem(lax.div(tile, 2), 2) + flip, 2)
+
+
 def kernel(
     sent, consts, surface, cot_surface, land_sea, bias, w_in_h, w_mid_h, w_out_h,
     out_f, out_g, g_in, g_mid, g_out, g_bias,
     w_in, w_mid, w_out, w_in_t, w_mid_t, w_out_t, sv, cv, mv, bv, flat, bmat,
     pre, hgt, dbr, a_s, b_s, ra, rb, hs, hr, st, br, xs, a1, a2, s1, s2, inc, ginc,
-    f_s, f_r, o_s, o_r, gacc, gs0, gs1, gr0, gr1, near0, near1, far0, far1, ag0, ag1,
+    f_s, f_r, o_s, o_r, gacc, gs0, gs1, mr0, mr1, cs0, cs1, gr0, gr1, near0, near1, far0, far1, ag0, ag1,
     sems, hsem, wsem,
 ):
     lev, tile, sec = (lax.axis_index(a) for a in EVERY)
-    r = lax.rem(lev, 2)
+    r = row_of(lev, tile)
     me_g = lev * 2 + sec
     spot = lax.rem(tile, 8)
     z_lo = lax.div(tile, 8)
@@ -53,8 +62,10 @@
     pos = lax.rem(z_lo, 4)
     quad = lax.div(z_lo, 4)
     me_f = sec * 2 + quad
-    sample = lax.div(lev, 2) * 2 + sec
-    gs, gr, near, far, ag = (gs0, gs1), (gr0, gr1), (near0, near1), (far0, far1), (ag0, ag1)
+    half_of = sample_half(lev, tile)
+    sample = half_of * 2 + sec
+    my_slot = (half_of * 2 + r) * 2 + sec
+    gs, mr, cs, gr, near, far, ag = (gs0, gs1), (mr0, mr1), (cs0, cs1), (gr0, gr1), (near0, near1), (far0, far1), (ag0, ag1)
 
     def of_group(q):
         return (lax.div(q, 2), tile, lax.rem(q, 2))
@@ -69,8 +80,13 @@
     def of_far(q):
         return (lev, (lax.rem(q, 2) * 4 + pos) * 8 + spot, lax.div(q, 2))
 
-    above = (lev + 1 - 2 * r, lax.rem(tile + r, TILES), sec)
-    below_dev = (lev + 1 - 2 * r, lax.rem(tile + TILES - 1 + r, TILES), sec)
+    def slot(q):
+        their = lax.div(q, 2)
+        return (sample_half(their, tile) * 2 + row_of(their, tile)) * 2 + lax.rem(q, 2)
+
+    partner = lax.rem(lev + 5 - 2 * r, 4)
+    above = (lev + (1 - r) * (partner - lev), lax.rem(tile + r, TILES), sec)
+    below_dev = (lev + r * (partner - lev), lax.rem(tile + TILES - 1 + r, TILES), sec)
 
     fetches = [
         pltpu.make_async_copy(src, dst, wsem.at[i])
@@ -99,7 +115,8 @@
     each(GROUP, me_g, lambda q: greet(of_group(q)))
     greet(above)
     greet(below_dev)
-    each(PLANE, me_p, lambda q: greet(of_plane(q)))
+    each(16, me_c, lambda q: greet(of_plane(core * 16 + q)))
+    greet(mate)
     each(4, pos, lambda q: greet(of_near(q)))
     each(4, me_f, lambda q: greet(of_far(q)))
 
@@ -118,7 +135,7 @@
         for base, dst in ((0, a_s), (24, b_s)):
             wide = sent[g, base : base + 24, :].astype(F32)
             pack(dst, g, wide[0:16], wide[16:24], nothing)
-    pl.semaphore_wait(barrier, GROUP - 1 + 2 + PLANE - 1 + 3 + 3)
+    pl.semaphore_wait(barrier, GROUP - 1 + 2 + 15 + 1 + 3 + 3)
 
     def push(src, dst, k, where):
         pushed.add(k)
@@ -139,10 +156,11 @@
     def leave():
         sizes = (
             ra.at[pl.ds(0, 7)], rb.at[pl.ds(0, 7)], f_r.at[pl.ds(0, 7)], o_r.at[pl.ds(0, 7)],
-            gr0.at[pl.ds(0, PLANE - 1)], gr1.at[pl.ds(0, PLANE - 1)], near0.at[pl.ds(0, 3)], near1.at[pl.ds(0, 3)],
+            mr0, mr1, near0.at[pl.ds(0, 3)], near1.at[pl.ds(0, 3)],
             far0.at[pl.ds(0, 3)], far1.at[pl.ds(0, 3)],
             ag0.at[pl.ds(0, 15 * SHARE[0])], ag1.at[pl.ds(0, 15 * SHARE[1])],
             ag0.at[pl.ds(0, 16 * SHARE[0])], ag1.at[pl.ds(0, 16 * SHARE[1])],
+            gr0.at[pl.ds(0, 15)], gr1.at[pl.ds(0, 15)],
         )
         for k in sorted(pushed):
             done(sizes[k], 2 * k)
@@ -154,8 +172,8 @@
                 if k not in halos_taken:
                     finish(hr.at[k, way], hsem.at[k, way, 1])
 
-    each(GROUP, me_g, lambda q: push(a_s.at[q], ra.at[me_g], 0, of_group(q)))
-    each(GROUP, me_g, lambda q: push(b_s.at[q], rb.at[me_g], 1, of_group(q)))
+    each(GROUP, me_g, lambda q: push(a_s.at[slot(q)], ra.at[me_g], 0, of_group(q)))
+    each(GROUP, me_g, lambda q: push(b_s.at[slot(q)], rb.at[me_g], 1, of_group(q)))
 
     lane = lax.broadcasted_iota(jnp.int32, (64, LANES), 1)
     real = lane < NLON
@@ -270,11 +288,11 @@
         for g in range(GROUP):
             u, v, t = (change[f * 64 + g * 8 : f * 64 + g * 8 + 8, :] for f in range(3))
             pack(src, g, jnp.concatenate([u, v], axis=0), t, tail)
-        dst[me_g] = src[me_g]
-        each(GROUP, me_g, lambda q: push(src.at[q], dst.at[me_g], k, of_group(q)))
-
-    ra[me_g] = a_s[me_g]
-    rb[me_g] = b_s[me_g]
+        dst[my_slot] = src[me_g]
+        each(GROUP, me_g, lambda q: push(src.at[q], dst.at[my_slot], k, of_group(q)))
+
+    ra[me_g] = a_s[my_slot]
+    rb[me_g] = b_s[my_slot]
     for copy in fetches:
         copy.wait()
     flat[...] = jnp.zeros_like(flat)
@@ -357,7 +375,15 @@
             gs[part][base : base + total.shape[0], :] = total[:, 128 * b : 128 * b + 128].astype(BF)
 
     def scatter(part):
-        each(PLANE, me_p, lambda q: push(share(gs[part], q, part), gr[part].at[me_p], 4 + part, of_plane(q)))
+        rows = 16 * SHARE[part]
+        push(gs[part].at[pl.ds(pl.multiple_of((1 - core) * rows, 16), rows)], mr[part], 4 + part, mate)
+
+    def combine(part):
+        done(mr[part], 2 * (4 + part) + 1)
+        rows = 16 * SHARE[part]
+        own = gs[part][pl.ds(pl.multiple_of(core * rows, 16), rows), :].astype(F32)
+        cs[part][...] = (own + mr[part][...].astype(F32)).astype(BF)
+        each(16, me_c, lambda q: push(share(cs[part], q, part), gr[part].at[me_c], 14 + part, of_plane(core * 16 + q)))
 
     gs1[3 * PART[1] :, :] = jnp.zeros((PLANE * SHARE[1] - 3 * PART[1], 128), BF)
     t1 = br[...].astype(BF)
@@ -370,7 +396,9 @@
     first_bar = (dot(w_mid[...], second_bar) * s1[0]).astype(BF)
     stage(gacc[576:784, :] + dot_last(xs[0], first_bar), 64, 1)
     scatter(1)
+    combine(0)
     input_bar = dot(w_in[...], first_bar).astype(BF).astype(F32)
+    combine(1)
 
     au, av, at_, asurf = adjoint(*halo_take(3))
     for i, d in enumerate((au, av, at_)):
@@ -379,22 +407,22 @@
     give(o_s, ginc, gsurf + asurf, o_r, 3)
 
     def sum_plane(part):
-        done(gr[part].at[pl.ds(0, PLANE - 1)], 2 * (4 + part) + 1)
-        mine = gs[part][pl.ds(pl.multiple_of(me_p * SHARE[part], 16), SHARE[part]), :].astype(F32)
+        done(gr[part].at[pl.ds(0, 15)], 2 * (14 + part) + 1)
+        mine = cs[part][pl.ds(pl.multiple_of(me_c * SHARE[part], 16), SHARE[part]), :].astype(F32)
         near[part][pos] = lax.fori_loop(
-            1, PLANE, lambda p, acc: acc + gr[part][lax.rem(me_p + p, PLANE)].astype(F32), mine
+            1, 16, lambda p, acc: acc + gr[part][lax.rem(me_c + p, 16)].astype(F32), mine
         )
         each(4, pos, lambda q: push(near[part].at[pos], near[part].at[pos], 6 + part, of_near(q)))
 
     def sum_near(part):
         done(near[part].at[pl.ds(0, 3)], 2 * (6 + part) + 1)
         n = near[part]
-        far[part][me_f] = ((n[0] + n[1]) + (n[2] + n[3])).astype(BF)
+        far[part][me_f] = (n[0] + n[1]) + (n[2] + n[3])
         each(4, me_f, lambda q: push(far[part].at[me_f], far[part].at[me_f], 8 + part, of_far(q)))
 
     def sum_far(part):
         done(far[part].at[pl.ds(0, 3)], 2 * (8 + part) + 1)
-        f = [far[part][i].astype(F32) for i in range(4)]
+        f = far[part]
         at = pl.ds(pl.multiple_of(me_p * SHARE[part], 16), SHARE[part])
         ag[part][at, :] = ((f[0] + f[1]) + (f[2] + f[3])).astype(BF)
         own = share(ag[part], me_p, part)
@@ -480,11 +508,13 @@
             v(slab, BF), v(slab, BF), v(slab, BF), v(slab, BF),
             v((GROWS, 384), F32),
             v((PLANE * SHARE[0], 128), BF), v((PLANE * SHARE[1], 128), BF),
-            v((PLANE, SHARE[0], 128), BF), v((PLANE, SHARE[1], 128), BF),
+            v((16 * SHARE[0], 128), BF), v((16 * SHARE[1], 128), BF),
+            v((16 * SHARE[0], 128), BF), v((16 * SHARE[1], 128), BF),
+            v((16, SHARE[0], 128), BF), v((16, SHARE[1], 128), BF),
             v((4, SHARE[0], 128), F32), v((4, SHARE[1], 128), F32),
-            v((4, SHARE[0], 128), BF), v((4, SHARE[1], 128), BF),
+            v((4, SHARE[0], 128), F32), v((4, SHARE[1], 128), F32),
             v((PLANE * SHARE[0], 128), BF), v((PLANE * SHARE[1], 128), BF),
-            pltpu.SemaphoreType.DMA((28,)), pltpu.SemaphoreType.DMA((4, 2, 2)), pltpu.SemaphoreType.DMA((7,)),
+            pltpu.SemaphoreType.DMA((32,)), pltpu.SemaphoreType.DMA((4, 2, 2)), pltpu.SemaphoreType.DMA((7,)),
         ],
         compiler_params=pltpu.CompilerParams(
             collective_id=0, has_side_effects=True, vmem_limit_bytes=40 * 2**20
@@ -495,8 +525,7 @@
 
 def on_device(fields, surface, cot_fields, cot_surface, land_sea, w_in, w_mid, w_out, bias_in):
     lev_i, tile_i = lax.axis_index("lev"), lax.axis_index("tile")
-    row_in_band = lax.rem(lev_i, 2)
-    row = tile_i * 2 + row_in_band
+    row = tile_i * 2 + row_of(lev_i, tile_i)
     latitude = -0.5 * math.pi + (row.astype(F32) + 0.5) * (math.pi / (2 * TILES))
     x_factor = 0.5 / jnp.maximum(jnp.cos(latitude), COS_FLOOR)
     sin_lat = jnp.sin(latitude)

time: 101 us -> 95.4 us (0.945)
  Pallas kernels: 90.6 us -> 84.5 us
    pallas_call x1, Pallas kernels: 90.6 us -> 84.5 us  [call(): pl.pallas_call(kernel, out_shape=(jax.ShapeDtypeStruct((GROUP, 32, LANES)...]
where the time goes in v5:
time: 95.4 us; the launch traced here: 95.2 us
  Pallas kernels  84.5 us (89%)
  local copies, waits for them, and re-layouts  5.23 us (5%)
  other arithmetic  4.42 us (5%)
  between operations  1.04 us (1%)
    pallas_call x1, Pallas kernels, call(): pl.pallas_call(kernel, out_shape=(jax.ShapeDtypeStruct((GROUP, 32, LANES)...  84.5 us
    unnamed x22, local copies, waits for them, and re-layouts  4.64 us

profile of v5, /device:TPU:1, one launch (start us, length us, event | category | flops | bytes accessed | tf_op | source)
XLA Modules:
  0.0 95.2 jit_solution(30505872220806313)
XLA Ops:
  0.8 0.1 concatenate.8
  0.9 0.1 broadcast_in_dim.2.consts
  1.0 0.0 copy-start.7
  1.0 1.1 %convert_element_type.20 = bf16[3,8,4,2,360]{4,3,2,1,0:T(2,128)(2,1)S(1)} convert(f32[3,8,4,2,360]{4,3,2,1,0:T(2,128)} %param.9) | non-fusion elementwise | flops 69120 | bytes 414720 | tf_op jit(solution)/shard_map/convert_element_type | solution.py:537
  2.2 0.0 copy-done.7
  2.2 0.2 multiply_convert_fusion
  2.3 0.0 copy-start.3
  2.3 0.0 copy-start.4
  2.3 0.0 copy-start.5
  2.4 0.0 copy-start.6
  2.4 0.0 copy-start
  2.4 0.0 copy-start.1
  2.4 0.0 copy-start.2
  2.5 0.6 copy-done.3
  3.0 0.0 copy-done.4
  3.1 0.0 copy-done.5
  3.1 0.0 copy-done.6
  3.1 0.3 copy-done
  3.4 0.0 copy-done.1
  3.4 0.1 copy-done.2
  3.5 84.5 %window.1 = (bf16[8,32,384]{2,1,0:T(8,128)(2,1)S(1)}, bf16[8,32,384]{2,1,0:T(8,128)(2,1)S(1)}, f32[192,384]{1,0:T(8,128)S(1)}, f32[384,384]{1,0:T(8,128)S(1)}, f...) custom-call(bf16[8,48,384]{2,1,0:T(8,128)(2,1)S(1)} %fusion.2.sent, f32[8,384]{1,0:T(8,128)S(1)} %broadcast_in_dim.2.consts, ...), custom_call_target="tpu_custom_call" | custom-call | tf_op jit(solution)/shard_map/window/pallas_call | solution.py:485
  88.0 0.1 slice_convert_fusion
  88.1 0.2 copy.21
  88.3 0.9 add.46
  89.2 0.6 bitcast_add_fusion
  89.9 0.0 copy-start.8
  89.9 0.2 copy.19
  90.0 0.8 copy-done.8
  90.8 0.9 add.42
  91.7 0.6 bitcast_add_fusion.1
  92.3 0.7 copy.29
  93.1 0.8 copy.30
  93.9 0.7 copy.31
  94.6 0.6 copy.32
  (11 shorter events, 0.2 us)
Async XLA Ops:
  1.0 1.1 %copy-start.7 = (f32[3,8,4,2,360]{4,3,2,1,0:T(2,128)S(1)}, f32[3,8,4,2,360]{4,3,2,1,0:T(2,128)}, u32[]{:S(2)}) copy-start(f32[3,8,4,2,360]{4,3,2,1,0:T(2,128)} %param.11) | copy-start | bytes 829444
  2.3 0.7 copy-start.3
  2.3 0.7 copy-start.4
  2.3 0.7 copy-start.5
  2.4 0.7 copy-start.6
  2.4 1.0 %copy-start = (bf16[384,384]{1,0:T(8,128)(2,1)S(1)}, bf16[384,384]{1,0:T(8,128)(2,1)}, u32[]{:S(2)}) copy-start(bf16[384,384]{1,0:T(8,128)(2,1)} %w_mid_h.1) | copy-start | bytes 884740
  2.4 1.0 %copy-start.1 = (bf16[192,384]{1,0:T(8,128)(2,1)S(1)}, bf16[192,384]{1,0:T(8,128)(2,1)}, u32[]{:S(2)}) copy-start(bf16[192,384]{1,0:T(8,128)(2,1)} %w_in_h.1) | copy-start | bytes 442372
  2.4 1.1 %copy-start.2 = (bf16[384,192]{0,1:T(8,128)(2,1)S(1)}, bf16[384,192]{0,1:T(8,128)(2,1)}, u32[]{:S(2)}) copy-start(bf16[384,192]{0,1:T(8,128)(2,1)} %param.16) | copy-start | bytes 442372
  89.9 1.0 %copy-start.8 = (f32[3,8,4,2,360]{4,3,2,1,0:T(2,128)S(1)}, f32[3,8,4,2,360]{4,3,2,1,0:T(2,128)}, u32[]{:S(2)}) copy-start(f32[3,8,4,2,360]{4,3,2,1,0:T(2,128)} %param.9) | copy-start | bytes 829444

commit v6 on v5

--- a/solution.py
+++ b/solution.py
@@ -277,7 +277,7 @@
             jnp.sum(hb, axis=0, keepdims=True),
         )
 
-    def give(src, change, surf_change, dst, k):
+    def lay_out(src, change, surf_change, dst):
         high = surf_change.astype(BF)
         low = (surf_change - high.astype(F32)).astype(BF)
         rows = lax.broadcasted_iota(jnp.int32, (8, 128), 0)
@@ -289,6 +289,8 @@
             u, v, t = (change[f * 64 + g * 8 : f * 64 + g * 8 + 8, :] for f in range(3))
             pack(src, g, jnp.concatenate([u, v], axis=0), t, tail)
         dst[my_slot] = src[me_g]
+
+    def give(src, dst, k):
         each(GROUP, me_g, lambda q: push(src.at[q], dst.at[my_slot], k, of_group(q)))
 
     ra[me_g] = a_s[my_slot]
@@ -361,7 +363,8 @@
     for i, d in enumerate((du, dv, dt)):
         at = slice(64 * i, 64 * i + 64)
         inc[at, :] = inc[at, :] + TIME_STEP * (d + tend[at])
-    give(f_s, inc, surf_inc + TIME_STEP * dsurf, f_r, 2)
+    lay_out(f_s, inc, surf_inc + TIME_STEP * dsurf, f_r)
+    give(f_s, f_r, 2)
 
     for at, g in gradients(1, t0, second_bar, first_bar):
         gacc[at : at + g.shape[0], :] = g
@@ -404,7 +407,7 @@
     for i, d in enumerate((au, av, at_)):
         at = slice(64 * i, 64 * i + 64)
         ginc[at, :] = ginc[at, :] + d + input_bar[at]
-    give(o_s, ginc, gsurf + asurf, o_r, 3)
+    lay_out(o_s, ginc, gsurf + asurf, o_r)
 
     def sum_plane(part):
         done(gr[part].at[pl.ds(0, 15)], 2 * (14 + part) + 1)
@@ -438,9 +441,7 @@
     sum_plane(1)
     sum_near(0)
     sum_near(1)
-    sum_far(0)
-    sum_far(1)
-
+    give(o_s, o_r, 3)
     def columns_out(came, out):
         for g in range(GROUP):
             u, v, t, rest = unpack(came[g].astype(F32))
@@ -450,16 +451,17 @@
             tail = jnp.where(row == 0, high, jnp.where(row == 1, low, 0.0))
             out[g] = jnp.concatenate([u, v, t, tail], axis=0).astype(BF)
 
-    to_mate(0)
     done(f_r.at[pl.ds(0, 7)], 5)
     columns_out(f_r, out_f)
+    sum_far(0)
+    sum_far(1)
+
+    to_mate(0)
     to_mate(1)
-    done(o_r.at[pl.ds(0, 7)], 7)
-    columns_out(o_r, out_g)
 
     def taken_from(part, b, first, last):
         base = PART[part] * b
-        return ag[part][base + first : base + last, :].astype(F32)
+        return ag[part][base + first : base + last, :]
 
     done(ag0.at[pl.ds(0, 16 * SHARE[0])], 25)
     for b in range(3):
@@ -471,7 +473,9 @@
         lanes = slice(128 * b, 128 * b + 128)
         g_mid[320:384, lanes] = taken_from(1, b, 0, 64)
         g_in[:, lanes] = taken_from(1, b, 64, 256)
-        g_bias[:, lanes] = taken_from(1, b, 256, 272)[0:2]
+        g_bias[:, lanes] = taken_from(1, b, 256, 272)
+    done(o_r.at[pl.ds(0, 7)], 7)
+    columns_out(o_r, out_g)
     leave()
 
 
@@ -487,10 +491,10 @@
         out_shape=(
             jax.ShapeDtypeStruct((GROUP, 32, LANES), BF),
             jax.ShapeDtypeStruct((GROUP, 32, LANES), BF),
-            jax.ShapeDtypeStruct((192, 384), F32),
-            jax.ShapeDtypeStruct((384, 384), F32),
-            jax.ShapeDtypeStruct((192, 384), F32),
-            jax.ShapeDtypeStruct((2, 384), F32),
+            jax.ShapeDtypeStruct((192, 384), BF),
+            jax.ShapeDtypeStruct((384, 384), BF),
+            jax.ShapeDtypeStruct((192, 384), BF),
+            jax.ShapeDtypeStruct((16, 384), BF),
         ),
         in_specs=[vmem] * 2 + [hbm] * 7,
         out_specs=tuple([vmem] * 6),
@@ -517,7 +521,7 @@
             pltpu.SemaphoreType.DMA((32,)), pltpu.SemaphoreType.DMA((4, 2, 2)), pltpu.SemaphoreType.DMA((7,)),
         ],
         compiler_params=pltpu.CompilerParams(
-            collective_id=0, has_side_effects=True, vmem_limit_bytes=40 * 2**20
+            collective_id=0, has_side_effects=True, vmem_limit_bytes=24 * 2**20
         ),
         name="window",
     )(*operands)
@@ -557,10 +561,10 @@
         surface + ds,
         cot_fields + dg,
         cot_surface + dgs,
-        g_in,
-        g_mid,
-        g_out.T,
-        g_bias,
+        g_in.astype(F32),
+        g_mid.astype(F32),
+        g_out.T.astype(F32),
+        g_bias[:2].astype(F32),
     )
 
 

time: 95.4 us -> 97.2 us (1.019)
  the two profiles are of different devices: /device:TPU:1 before, /device:TPU:33 now
where the time goes in v6:
time: 97.2 us; the launch traced here: 97 us
  Pallas kernels  86.6 us (89%)
  other arithmetic  7.34 us (8%)
  local copies, waits for them, and re-layouts  2 us (2%)
  between operations  1.05 us (1%)
    pallas_call x1, Pallas kernels, call(): pl.pallas_call(kernel, out_shape=(jax.ShapeDtypeStruct((GROUP, 32, LANES)...  86.6 us

profile of v6, /device:TPU:33, one launch (start us, length us, event | category | flops | bytes accessed | tf_op | source)
XLA Modules:
  0.0 97.0 jit_solution(11112544617318739455)
XLA Ops:
  0.6 0.0 copy-start.7
  0.6 1.2 %multiply_convert_fusion = bf16[3,8,4,2,360]{4,3,2,1,0:T(2,128)(2,1)S(1)} fusion(f32[3,8,4,2,360]{4,3,2,1,0:T(2,128)} %param.11), kind=kLoop, calls=%fused_computation.6 | loop fusion | flops 138240 | bytes 414720 | tf_op jit(solution)/shard_map/convert_element_type | solution.py:541
  1.8 0.0 copy-done.7
  1.8 0.1 convert_element_type.35
  2.0 0.0 copy-start
  2.0 0.0 copy-start.1
  2.0 0.0 copy-start.2
  2.1 0.0 copy-start.5
  2.1 0.0 copy-start.6
  2.3 0.0 copy-start.3
  2.3 0.0 copy-start.4
  2.3 0.1 concatenate.8
  2.4 0.1 broadcast_in_dim.2.consts
  2.5 0.5 copy-done
  2.9 0.0 copy-done.1
  3.0 0.1 copy-done.2
  3.1 0.0 copy-done.5
  3.1 0.0 copy-done.6
  3.1 0.0 copy-done.3
  3.1 0.0 copy-done.4
  3.1 86.6 %window.1 = (bf16[8,32,384]{2,1,0:T(8,128)(2,1)S(1)}, bf16[8,32,384]{2,1,0:T(8,128)(2,1)S(1)}, bf16[192,384]{1,0:T(8,128)(2,1)S(1)}, bf16[384,384]{1,0:T(8,128)(...) custom-call(bf16[8,48,384]{2,1,0:T(8,128)(2,1)S(1)} %fusion.2.sent, ...), custom_call_target="tpu_custom_call" | custom-call | tf_op jit(solution)/shard_map/window/pallas_call | solution.py:489
  89.7 0.1 slice_convert_fusion
  89.8 0.2 copy.19
  90.0 0.9 add.42
  90.9 0.6 bitcast_add_fusion.1
  91.6 0.0 copy-start.8
  91.6 0.2 copy.21
  91.7 0.8 copy-done.8
  92.5 0.9 add.46
  93.5 0.6 bitcast_add_fusion
  94.1 0.7 convert_element_type.40
  94.8 0.9 convert_element_type.41
  95.7 0.7 convert_bitcast_fusion
  96.4 0.6 slice_convert_fusion.2
  (11 shorter events, 0.2 us)
Async XLA Ops:
  0.6 1.2 %copy-start.7 = (f32[3,8,4,2,360]{4,3,2,1,0:T(2,128)S(1)}, f32[3,8,4,2,360]{4,3,2,1,0:T(2,128)}, u32[]{:S(2)}) copy-start(f32[3,8,4,2,360]{4,3,2,1,0:T(2,128)} %param.9) | copy-start | bytes 829444
  2.0 1.0 copy-start
  2.0 1.0 %copy-start.1 = (bf16[192,384]{1,0:T(8,128)(2,1)S(1)}, bf16[192,384]{1,0:T(8,128)(2,1)}, u32[]{:S(2)}) copy-start(bf16[192,384]{1,0:T(8,128)(2,1)} %w_in_h.1) | copy-start | bytes 442372
  2.0 1.0 %copy-start.2 = (bf16[384,192]{0,1:T(8,128)(2,1)S(1)}, bf16[384,192]{0,1:T(8,128)(2,1)}, u32[]{:S(2)}) copy-start(bf16[384,192]{0,1:T(8,128)(2,1)} %param.16) | copy-start | bytes 442372
  2.1 1.0 %copy-start.5 = (s32[2,360]{1,0:T(2,128)S(1)}, s32[2,360]{1,0:T(2,128)}, u32[]{:S(2)}) copy-start(s32[2,360]{1,0:T(2,128)} %land_sea.1) | copy-start | bytes 8644
  2.1 1.0 %copy-start.6 = (f32[2,384]{1,0:T(2,128)S(1)}, f32[2,384]{1,0:T(2,128)}, u32[]{:S(2)}) copy-start(f32[2,384]{1,0:T(2,128)} %bias.1) | copy-start | bytes 9220
  2.3 0.8 copy-start.3
  2.3 0.8 copy-start.4
  91.6 1.0 copy-start.8

commit v7 on v6

--- a/solution.py
+++ b/solution.py
@@ -277,7 +277,7 @@
             jnp.sum(hb, axis=0, keepdims=True),
         )
 
-    def lay_out(src, change, surf_change, dst):
+    def give(src, change, surf_change, dst, k):
         high = surf_change.astype(BF)
         low = (surf_change - high.astype(F32)).astype(BF)
         rows = lax.broadcasted_iota(jnp.int32, (8, 128), 0)
@@ -289,8 +289,6 @@
             u, v, t = (change[f * 64 + g * 8 : f * 64 + g * 8 + 8, :] for f in range(3))
             pack(src, g, jnp.concatenate([u, v], axis=0), t, tail)
         dst[my_slot] = src[me_g]
-
-    def give(src, dst, k):
         each(GROUP, me_g, lambda q: push(src.at[q], dst.at[my_slot], k, of_group(q)))
 
     ra[me_g] = a_s[my_slot]
@@ -359,13 +357,6 @@
     dbr[...] = div_bar(sbar1)
     halo_send(3, br[64:128, :], dbr[...])
 
-    du, dv, dt, dsurf = dynamics(*halo_take(2))
-    for i, d in enumerate((du, dv, dt)):
-        at = slice(64 * i, 64 * i + 64)
-        inc[at, :] = inc[at, :] + TIME_STEP * (d + tend[at])
-    lay_out(f_s, inc, surf_inc + TIME_STEP * dsurf, f_r)
-    give(f_s, f_r, 2)
-
     for at, g in gradients(1, t0, second_bar, first_bar):
         gacc[at : at + g.shape[0], :] = g
 
@@ -407,7 +398,14 @@
     for i, d in enumerate((au, av, at_)):
         at = slice(64 * i, 64 * i + 64)
         ginc[at, :] = ginc[at, :] + d + input_bar[at]
-    lay_out(o_s, ginc, gsurf + asurf, o_r)
+    give(o_s, ginc, gsurf + asurf, o_r, 3)
+
+    du, dv, dt, dsurf = dynamics(*halo_take(2))
+    for i, d in enumerate((du, dv, dt)):
+        at = slice(64 * i, 64 * i + 64)
+        inc[at, :] = inc[at, :] + TIME_STEP * (d + tend[at])
+    give(f_s, inc, surf_inc + TIME_STEP * dsurf, f_r, 2)
+
 
     def sum_plane(part):
         done(gr[part].at[pl.ds(0, 15)], 2 * (14 + part) + 1)
@@ -441,7 +439,9 @@
     sum_plane(1)
     sum_near(0)
     sum_near(1)
-    give(o_s, o_r, 3)
+    sum_far(0)
+    sum_far(1)
+
     def columns_out(came, out):
         for g in range(GROUP):
             u, v, t, rest = unpack(came[g].astype(F32))
@@ -451,13 +451,12 @@
             tail = jnp.where(row == 0, high, jnp.where(row == 1, low, 0.0))
             out[g] = jnp.concatenate([u, v, t, tail], axis=0).astype(BF)
 
+    to_mate(0)
     done(f_r.at[pl.ds(0, 7)], 5)
     columns_out(f_r, out_f)
-    sum_far(0)
-    sum_far(1)
-
-    to_mate(0)
     to_mate(1)
+    done(o_r.at[pl.ds(0, 7)], 7)
+    columns_out(o_r, out_g)
 
     def taken_from(part, b, first, last):
         base = PART[part] * b
@@ -474,8 +473,6 @@
         g_mid[320:384, lanes] = taken_from(1, b, 0, 64)
         g_in[:, lanes] = taken_from(1, b, 64, 256)
         g_bias[:, lanes] = taken_from(1, b, 256, 272)
-    done(o_r.at[pl.ds(0, 7)], 7)
-    columns_out(o_r, out_g)
     leave()
 
 
@@ -521,7 +518,7 @@
             pltpu.SemaphoreType.DMA((32,)), pltpu.SemaphoreType.DMA((4, 2, 2)), pltpu.SemaphoreType.DMA((7,)),
         ],
         compiler_params=pltpu.CompilerParams(
-            collective_id=0, has_side_effects=True, vmem_limit_bytes=24 * 2**20
+            collective_id=0, has_side_effects=True, vmem_limit_bytes=40 * 2**20
         ),
         name="window",
     )(*operands)

time: 97.2 us -> 99.7 us (1.026)
  the two profiles are of different devices: /device:TPU:33 before, /device:TPU:1 now
where the time goes in v7:
time: 99.7 us; the launch traced here: 99.5 us
  Pallas kernels  89.1 us (89%)
  other arithmetic  7.34 us (7%)
  local copies, waits for them, and re-layouts  2 us (2%)
  between operations  1.05 us (1%)
    pallas_call x1, Pallas kernels, call(): pl.pallas_call(kernel, out_shape=(jax.ShapeDtypeStruct((GROUP, 32, LANES)...  89.1 us

profile of v7, /device:TPU:1, one launch (start us, length us, event | category | flops | bytes accessed | tf_op | source)
XLA Modules:
  0.0 99.5 jit_solution(12910830602320894859)
XLA Ops:
  0.6 0.0 copy-start.7
  0.6 1.2 %multiply_convert_fusion = bf16[3,8,4,2,360]{4,3,2,1,0:T(2,128)(2,1)S(1)} fusion(f32[3,8,4,2,360]{4,3,2,1,0:T(2,128)} %param.11), kind=kLoop, calls=%fused_computation.6 | loop fusion | flops 138240 | bytes 414720 | tf_op jit(solution)/shard_map/convert_element_type | solution.py:538
  1.8 0.0 copy-done.7
  1.8 0.1 convert_element_type.35
  2.0 0.0 copy-start
  2.0 0.0 copy-start.1
  2.0 0.0 copy-start.2
  2.1 0.0 copy-start.5
  2.1 0.0 copy-start.6
  2.3 0.0 copy-start.3
  2.3 0.0 copy-start.4
  2.3 0.1 concatenate.8
  2.4 0.1 broadcast_in_dim.2.consts
  2.5 0.5 copy-done
  2.9 0.0 copy-done.1
  3.0 0.1 copy-done.2
  3.1 0.0 copy-done.5
  3.1 0.0 copy-done.6
  3.1 0.0 copy-done.3
  3.1 0.0 copy-done.4
  3.1 89.1 %window.1 = (bf16[8,32,384]{2,1,0:T(8,128)(2,1)S(1)}, bf16[8,32,384]{2,1,0:T(8,128)(2,1)S(1)}, bf16[192,384]{1,0:T(8,128)(2,1)S(1)}, bf16[384,384]{1,0:T(8,128)(...) custom-call(bf16[8,48,384]{2,1,0:T(8,128)(2,1)S(1)} %fusion.2.sent, ...), custom_call_target="tpu_custom_call" | custom-call | tf_op jit(solution)/shard_map/window/pallas_call | solution.py:486
  92.2 0.1 slice_convert_fusion
  92.3 0.2 copy.19
  92.4 0.9 add.42
  93.4 0.6 bitcast_add_fusion.1
  94.0 0.0 copy-start.8
  94.1 0.2 copy.21
  94.2 0.8 copy-done.8
  95.0 0.9 add.46
  96.0 0.6 bitcast_add_fusion
  96.6 0.7 convert_element_type.40
  97.3 0.9 convert_element_type.41
  98.2 0.7 convert_bitcast_fusion
  98.9 0.6 slice_convert_fusion.2
  (11 shorter events, 0.2 us)
Async XLA Ops:
  0.6 1.2 %copy-start.7 = (f32[3,8,4,2,360]{4,3,2,1,0:T(2,128)S(1)}, f32[3,8,4,2,360]{4,3,2,1,0:T(2,128)}, u32[]{:S(2)}) copy-start(f32[3,8,4,2,360]{4,3,2,1,0:T(2,128)} %param.9) | copy-start | bytes 829444
  2.0 1.0 copy-start
  2.0 1.0 copy-start.1
  2.0 1.0 %copy-start.2 = (bf16[384,192]{0,1:T(8,128)(2,1)S(1)}, bf16[384,192]{0,1:T(8,128)(2,1)}, u32[]{:S(2)}) copy-start(bf16[384,192]{0,1:T(8,128)(2,1)} %param.16) | copy-start | bytes 442372
  2.1 1.0 copy-start.5
  2.1 1.0 copy-start.6
  2.3 0.8 copy-start.3
  2.3 0.8 copy-start.4
  94.0 1.0 copy-start.8
